TPU v7x, 32 devices: a whole 2x2x4 slice. The times are simulated.
32 devices in a mesh: groups: 2 (over y), pool: 8 (over z, core), tensor: 2 (over x).
Axes of the slice: x: 2, y: 2, z: 4, core: 2. Of those that a mesh axis runs over, the one named last changes fastest.
Arguments:
- tokens: bfloat16 [4096, 12288], P(('groups', 'pool'), 'tensor'), parts along dimension 0, may hold values from -6 to 6
- tenant_ids: int32 [4096], P(('groups', 'pool')), parts along dimension 0, may hold values from 0 to 127, as said below
- slot_table: int32 [256], P('groups'), parts along dimension 0, may hold values from 0 to 127, as said below
- value_weight: bfloat16 [12288, 1024], P('tensor', 'pool'), may hold values from -0.0546875 to 0.0546875
- low_a: bfloat16 [12288, 4096], P('tensor', ('groups', 'pool')), parts along dimension 1, may hold values from -0.0546875 to 0.0546875
- low_b: bfloat16 [4096, 1024], P(('groups', 'pool')), parts along dimension 0, may hold values from -1.5 to 1.5
- tile_data: bfloat16 [256, 4, 128, 128], P(('groups', 'pool'), 'tensor'), parts along dimension 0, may hold values from -0.5 to 0.5
- tile_pos: int32 [256, 4], P(('groups', 'pool'), 'tensor'), parts along dimension 0, may hold values from 0 to 383
Outputs:
- values: bfloat16 [4096, 1024], P(('groups', 'pool'), 'tensor'), parts along dimension 0
There are 2 independent parts, one for each index of `groups`. A program takes and returns all parts, laid end to end along the dimension named above; an argument that names none is the same for every part. Nothing has to cross between parts.
Inputs may be any that keep to these rules, and one draw needn't show every extreme that they name: A permutation: tenant t's adapter lies in slot slot_table[t], held by pool index slot_table[t] // 16. `tenant_ids`: among the 256 tokens of one pool index, at most 64 have tenants whose slots lie with one pool index; some pool index receives exactly 64 from every pool index.
All inputs are finite; a program needn't handle non-finite values.
Results may differ from a plain program's by a relative error of at most 0.001.
Values may be sent and summed in bfloat16 or wider, within the bound.
A program may use at most 128 MiB of HBM per device.

v0:
```python
import jax
import jax.numpy as jnp
from jax import lax
from jax.sharding import PartitionSpec as P

RANK = 16


def owner_terms(row_feats, row_tags, low_a, low_b, tile_data, tile_pos):
    row_total, features = row_feats.shape
    slots_here = low_b.shape[0] // RANK
    tile_side = tile_data.shape[-1]
    per_shard = tile_pos.shape[1]
    blocks_here = features // tile_side
    col_count = low_b.shape[1] // tile_side
    slot_mask = (row_tags[:, None] == jnp.arange(1, slots_here + 1)[None, :]).astype(jnp.float32)
    coeff = jnp.dot(row_feats, low_a, preferred_element_type=jnp.float32)
    coeff = coeff * jnp.repeat(slot_mask, RANK, axis=1)
    low_rank = jnp.dot(coeff, low_b.astype(jnp.float32), precision=lax.Precision.HIGHEST)
    flat_pos = tile_pos.reshape(-1)
    row_block = flat_pos // col_count
    col_block = flat_pos % col_count
    picked = jnp.take(row_feats.reshape(row_total, blocks_here, tile_side), row_block, axis=1)
    products = jnp.einsum(
        "ntf,tfg->ntg",
        picked,
        tile_data.reshape(-1, tile_side, tile_side),
        preferred_element_type=jnp.float32,
    )
    tile_mask = jnp.repeat(slot_mask, per_shard, axis=1)
    placing = (col_block[:, None] == jnp.arange(col_count)[None, :]).astype(jnp.float32)
    sparse = jnp.einsum(
        "ntg,tc->ncg", products * tile_mask[:, :, None], placing, precision=lax.Precision.HIGHEST
    )
    return low_rank + sparse.reshape(row_total, col_count * tile_side)


def local(tokens, tenant_ids, slot_table, value_weight, low_a, low_b, tile_data, tile_pos):
    local_rows, features = tokens.shape
    pool_width = lax.axis_size("pool")
    slots_here = low_b.shape[0] // RANK
    capacity = 2 * local_rows // pool_width
    match_table = tenant_ids[:, None] == jnp.arange(slot_table.shape[0])[None, :]
    slot = jnp.sum(jnp.where(match_table, slot_table[None, :], 0), axis=1)
    holder = slot // slots_here
    local_slot = slot % slots_here
    holder_hits = (holder[:, None] == jnp.arange(pool_width)[None, :]).astype(jnp.int32)
    position = jnp.sum((jnp.cumsum(holder_hits, axis=0) - 1) * holder_hits, axis=1)
    destination = holder * capacity + position
    send_rows = (
        jnp.zeros((pool_width * capacity, features), jnp.bfloat16).at[destination].set(tokens)
    )
    send_tags = jnp.zeros((pool_width * capacity,), jnp.int32).at[destination].set(local_slot + 1)
    recv_rows, recv_tags = (
        lax.all_to_all(
            send_rows.reshape(pool_width, capacity, features),
            "pool",
            split_axis=0,
            concat_axis=0,
            tiled=True,
        ),
        lax.all_to_all(
            send_tags.reshape(pool_width, capacity), "pool", split_axis=0, concat_axis=0, tiled=True
        ),
    )
    delta = owner_terms(
        recv_rows.reshape(-1, features), recv_tags.reshape(-1), low_a, low_b, tile_data, tile_pos
    )
    base = jnp.dot(
        tokens,
        lax.all_gather(value_weight, "pool", axis=1, tiled=True),
        preferred_element_type=jnp.float32,
    )
    returned = lax.all_to_all(
        delta.reshape(pool_width, capacity, -1), "pool", split_axis=0, concat_axis=0, tiled=True
    )
    own_terms = jnp.take(returned.reshape(pool_width * capacity, -1), destination, axis=0)
    to_reduce = base + own_terms
    summed = lax.psum_scatter(to_reduce, "tensor", scatter_dimension=1, tiled=True)
    return summed.astype(jnp.bfloat16)


def solution(mesh):
    return jax.shard_map(
        local,
        mesh=mesh,
        in_specs=(
            P(("groups", "pool"), "tensor"),
            P(("groups", "pool")),
            P("groups"),
            P("tensor", "pool"),
            P("tensor", ("groups", "pool")),
            P(("groups", "pool"), None),
            P(("groups", "pool"), "tensor", None, None),
            P(("groups", "pool"), "tensor"),
        ),
        out_specs=P(("groups", "pool"), "tensor"),
        check_vma=False,
    )
```

profile of v0, /device:TPU:0, one launch (start us, length us, event | category | flops | bytes accessed | tf_op | source)
XLA Modules:
  0.0 387.8 jit_solution(2431717160078936893)
XLA Ops:
  6.5 0.7 all-gather.2.cloned.1.call-update
  7.3 1.1 select_reduce_fusion
  8.4 0.6 reduce-window.6
  9.0 0.2 slice_reduce_fusion
  9.2 0.1 fusion.11
  9.3 1.4 scatter_custom_fusion.1
  10.8 0.7 all_to_all.13
  11.4 6.3 %all-to-all-start.1 = ((s32[8,1,64]{2,1,0:T(1,128)}), s32[8,1,64]{2,1,0:T(1,128)S(1)}, u32[]{:S(2)}, u32[]{:S(2)}) async-start(s32[8,1,64]{2,1,0:T(1,128)} %all_to_all.13), calls=%async_computation.1 | async-start | bytes 8192 | tf_op jit(solution)/shard_map/all_to_all | solution.py:62
  17.8 10.1 %scatter_custom_fusion = bf16[512,6144]{1,0:T(8,128)(2,1)} fusion(s32[256]{0:T(256)S(1)} %bitcast.61, bf16[256,6144]{1,0:T(8,128)(2,1)} %param.8, bf16[]{:T(256)} %constant.90.clone.1), kind=kCustom, calls=%fused_computation.11 | custom fusion | bytes 6291968 | tf_op jit(solution)/shard_map/scatter | solution.py:51
  27.9 5.2 %all-to-all-start = ((bf16[8,64,6144]{2,1,0:T(8,128)(2,1)}), bf16[8,64,6144]{2,1,0:T(8,128)(2,1)}, u32[]{:S(2)}, u32[]{:S(2)}) async-start(bf16[8,64,6144]{2,1,0:T(8,128)(2,1)} %bitcast.52), calls=%async_computation | async-start | bytes 12582912 | tf_op jit(solution)/shard_map/all_to_all | solution.py:55
  33.1 0.1 copy.20
  33.2 0.1 reshape.245
  33.3 0.1 reshape.244
  33.5 0.5 broadcast.366
  34.0 0.7 reduce.5
  34.9 0.9 broadcast_in_dim.59
  35.8 2.1 copy.19
  37.9 223.3 %all-to-all-done = bf16[8,64,6144]{2,1,0:T(8,128)(2,1)} async-done(((bf16[8,64,6144]{2,1,0:T(8,128)(2,1)}), bf16[8,64,6144]{2,1,0:T(8,128)(2,1)}, u32[]{:S(2)}, u32[]{:S(2)}) %all-to-all-start) | async-done | bytes 6291488 | tf_op jit(solution)/shard_map/all_to_all | solution.py:55
  261.1 4.7 %copy.24 = bf16[64,8,48,128]{3,2,1,0:T(8,128)(2,1)S(1)} copy(bf16[64,8,48,128]{3,1,2,0:T(8,128)(2,1)} %bitcast.19) | data formatting | bytes 12582912
  265.8 4.2 %copy.22 = bf16[512,48,128]{2,0,1:T(8,128)(2,1)} copy(bf16[512,48,128]{2,1,0:T(8,128)(2,1)S(1)} %bitcast.53) | data formatting | bytes 12582912 | tf_op jit(solution)/shard_map/reshape;reshape | solution.py:23
  270.0 5.8 %gather_fusion = bf16[32,512,128]{2,1,0:T(8,128)(2,1)} fusion(bf16[512,48,128]{2,0,1:T(8,128)(2,1)} %copy.22, s32[1024]{0:T(1024)S(1)} %pad_clamp_fusion.1), kind=kCustom, calls=%fused_computation | custom fusion | bytes 8388736 | tf_op jit(solution)/shard_map/jit(_take)/gather | solution.py:23
  275.9 4.2 %bitcast_multiply_fusion = f32[512,32,128]{2,0,1:T(8,128)S(1)} fusion(f32[512,32]{0,1:T(8,128)S(1)} %mul.41, bf16[32,128,128]{2,1,0:T(8,128)(2,1)} %bitcast.57, bf16[32,512,128]{2,1,0:T(8,128)(2,1)} %gather_fusion, pred[32]{0:T(512)(128)(4,1)S(1)} %compare_and_fusion), kind=kOutput, calls=%fused_computation.4 | convolution fusion | flops 541065216 | bytes 13697056 | tf_op jit(solution)/shard_map/ntf,tfg->ntg/dot_general | solution.py:24
  280.1 7.6 %fusion = f32[8,512,128]{2,0,1:T(8,128)S(1)} fusion(f32[512,32,128]{2,0,1:T(8,128)S(1)} %bitcast_multiply_fusion, s32[32]{0:T(128)S(1)} %and_select_fusion.3), kind=kOutput, calls=%fused_computation.5 | convolution fusion | flops 201326848 | bytes 10485888 | tf_op jit(solution)/shard_map/ntg,tc->ncg/dot_general | solution.py:32
  287.7 4.6 %convolution_multiply_fusion = f32[512,256]{1,0:T(8,128)S(1)} fusion(f32[512,256]{1,0:T(8,128)S(1)} %copy-done.3, bf16[512,6144]{1,0:T(8,128)(2,1)} %bitcast.7, bf16[6144,256]{1,0:T(8,128)(2,1)S(1)} %copy-done), kind=kOutput, calls=%fused_computation.16 | convolution fusion | flops 1610743808 | bytes 10485760 | tf_op jit(solution)/shard_map/dot_general | solution.py:17
  292.3 2.6 bitcast_add_fusion
  294.9 3.6 all-to-all-start.2
  298.5 0.3 reduce-scatter.2.cloned.1.call-start
  298.8 48.7 %all-to-all-done.2 = f32[8,64,1024]{2,1,0:T(8,128)S(1)} async-done(((f32[8,64,1024]{2,1,0:T(8,128)}), f32[8,64,1024]{2,1,0:T(8,128)S(1)}, u32[]{:S(2)}, u32[]{:S(2)}) %all-to-all-start.2) | async-done | bytes 2097184 | tf_op jit(solution)/shard_map/all_to_all | solution.py:74
  347.5 2.1 gather_fusion.1
  349.6 10.3 %convolution_add_fusion = f32[256,1024]{1,0:T(8,128)} fusion(bf16[256,6144]{1,0:T(8,128)(2,1)} %param.8, bf16[6144,1024]{1,0:T(8,128)(2,1)} %all-gather.2.cloned.1.call-done, f32[256,1024]{1,0:T(8,128)} %gather_fusion.1, pred[256]{0:T(512)(128)(4,1)S(1)} %compare_and_fusion.1), kind=kOutput, calls=%fused_computation.15 | convolution fusion | flops 3221749760 | bytes 17826048 | tf_op jit(solution)/shard_map/dot_general | solution.py:69
  359.9 19.3 %reduce-scatter.2.cloned.1.call-done = f32[256,512]{1,0:T(8,128)} async-done(((f32[256,1024]{1,0:T(8,128)}), f32[256,512]{1,0:T(8,128)}) %reduce-scatter.2.cloned.1.call-update) | async-done | bytes 524304 | tf_op jit(solution)/shard_map/reduce_scatter | solution.py:79
  379.2 1.8 convert_element_type.15
  (31 shorter events, 0.4 us)
Async XLA Ops:
  6.5 281.1 %copy-start = (bf16[6144,256]{1,0:T(8,128)(2,1)S(1)}, bf16[6144,256]{1,0:T(8,128)(2,1)}, u32[]{:S(2)}) copy-start(bf16[6144,256]{1,0:T(8,128)(2,1)} %param.12) | copy-start | bytes 9437188
  6.5 343.1 %all-gather.2.cloned.1.call-start = ((), (), s32[]{:S(2)}) async-start(), calls=%async_computation.4 | async-start | bytes 14155776 | tf_op jit(solution)/shard_map/all_gather | solution.py:71
  11.4 16.5 %all-to-all-start.1 = ((s32[8,1,64]{2,1,0:T(1,128)}), s32[8,1,64]{2,1,0:T(1,128)S(1)}, u32[]{:S(2)}, u32[]{:S(2)}) async-start(s32[8,1,64]{2,1,0:T(1,128)} %all_to_all.13), calls=%async_computation.1 | async-start | bytes 8192 | tf_op jit(solution)/shard_map/all_to_all | solution.py:62
  27.9 5.2 %copy-start.4 = (s32[16,2]{0,1:T(2,128)S(1)}, s32[16,2]{0,1:T(2,128)}, u32[]{:S(2)}) copy-start(s32[16,2]{0,1:T(2,128)} %param.15) | copy-start | bytes 388
  27.9 233.2 %all-to-all-start = ((bf16[8,64,6144]{2,1,0:T(8,128)(2,1)}), bf16[8,64,6144]{2,1,0:T(8,128)(2,1)}, u32[]{:S(2)}, u32[]{:S(2)}) async-start(bf16[8,64,6144]{2,1,0:T(8,128)(2,1)} %bitcast.52), calls=%async_computation | async-start | bytes 12582912 | tf_op jit(solution)/shard_map/all_to_all | solution.py:55
  280.1 7.6 %copy-start.3 = (f32[512,256]{1,0:T(8,128)S(1)}, f32[512,256]{1,0:T(8,128)}, u32[]{:S(2)}) copy-start(f32[512,256]{1,0:T(8,128)} %copy.19) | copy-start | bytes 1572868
  287.7 4.7 %copy-start.2 = (bf16[256,1024]{1,0:T(8,128)(2,1)S(1)}, bf16[256,1024]{1,0:T(8,128)(2,1)}, u32[]{:S(2)}) copy-start(bf16[256,1024]{1,0:T(8,128)(2,1)} %param.13) | copy-start | bytes 1572868
  294.9 52.6 %all-to-all-start.2 = ((f32[8,64,1024]{2,1,0:T(8,128)}), f32[8,64,1024]{2,1,0:T(8,128)S(1)}, u32[]{:S(2)}, u32[]{:S(2)}) async-start(f32[8,64,1024]{2,1,0:T(8,128)} %bitcast.54), calls=%async_computation.2 | async-start | bytes 4194304 | tf_op jit(solution)/shard_map/all_to_all | solution.py:74
  298.5 80.7 %reduce-scatter.2.cloned.1.call-start = ((), (), s32[]{:S(2)}) async-start(), calls=%async_computation.5 | async-start | bytes 1572864 | tf_op jit(solution)/shard_map/reduce_scatter | solution.py:79
  349.6 31.4 %copy-start.1 = (bf16[6144,256]{1,0:T(8,128)(2,1)S(1)}, bf16[6144,256]{1,0:T(8,128)(2,1)}, u32[]{:S(2)}) copy-start(bf16[6144,256]{1,0:T(8,128)(2,1)} %param.12) | copy-start | bytes 9437188
Sparse Core Ops, SparseCore 0:
  8.9 237.6 all-gather.1
  360.1 19.1 reduce-scatter.1
where the time goes:
time: 388 us
  waiting for transfers between devices  292 us (75%)
  local copies, waits for them, and re-layouts  33.2 us (9%)
  matrix products  29.3 us (8%)
  starting transfers between devices  15.4 us (4%)
  between operations  13.6 us (4%)
  other arithmetic  4.42 us (1%)
    all_to_all x1, waiting for transfers between devices, local(): lax.all_to_all(send_rows.reshape(pool_width, capacity, features), 'pool',...  223 us
    all_to_all x1, waiting for transfers between devices, local(): lax.all_to_all(delta.reshape(pool_width, capacity, -1), 'pool', split_axi...  48.7 us
    reduce_scatter x1, waiting for transfers between devices, local(): lax.psum_scatter(to_reduce, 'tensor', scatter_dimension=1, tiled=True)  19.3 us
    dot_general x1, matrix products, local(): jnp.dot(tokens, lax.all_gather(value_weight, 'pool', axis=1, tiled=True),...  10.3 us
    scatter x1, local copies, waits for them, and re-layouts, local(): jnp.zeros((pool_width * capacity, features), jnp.bfloat16).at[destination]  10.1 us
  transfers between devices with their start and end apart: 5, of which 3 were waited for; matrix products, arithmetic and copies ran while one was open for 14% of the time, Pallas kernels for 0%

commit v1 on v0

v1 whole, which is shorter than its diff:
```python
import jax
import jax.numpy as jnp
from jax import lax
from jax.sharding import PartitionSpec as P

RANK = 16
CHUNKS = 2


def split3(x):
    high = lax.reduce_precision(x, 8, 7)
    rest = x - high
    mid = lax.reduce_precision(rest, 8, 7)
    low = rest - mid
    return [part.astype(jnp.bfloat16) for part in (high, mid, low)]


def local(tokens, tenant_ids, slot_table, value_weight, low_a, low_b, tile_data, tile_pos):
    local_rows, features = tokens.shape
    pool_width = lax.axis_size("pool")
    tensor_width = lax.axis_size("tensor")
    group_width = lax.axis_size("groups")
    slots_here = low_b.shape[0] // RANK
    columns = low_b.shape[1]
    own_columns = columns // tensor_width
    tile_side = tile_data.shape[-1]
    per_shard = tile_pos.shape[1]
    col_count = columns // tile_side
    capacity = 2 * local_rows // pool_width
    slot_total = slot_table.shape[0]
    bf16 = jnp.bfloat16
    f32 = jnp.float32

    def exchange(x):
        return lax.all_to_all(x, "pool", split_axis=0, concat_axis=0, tiled=True)

    share = features // group_width
    group = lax.axis_index("groups")
    part_weight = lax.dynamic_slice_in_dim(value_weight, group * share, share, axis=0)
    near_weight = lax.all_gather(part_weight, "pool", axis=1, tiled=True)

    match_table = tenant_ids[:, None] == jnp.arange(slot_total)[None, :]
    slot = jnp.sum(jnp.where(match_table, slot_table[None, :], 0), axis=1)
    holder = slot // slots_here
    local_slot = slot % slots_here
    holder_hits = (holder[:, None] == jnp.arange(pool_width)[None, :]).astype(jnp.int32)
    earlier = (jnp.arange(local_rows)[:, None] >= jnp.arange(local_rows)[None, :]).astype(bf16)
    ranks = jnp.dot(earlier, holder_hits.astype(bf16), preferred_element_type=f32).astype(jnp.int32)
    position = jnp.sum((ranks - 1) * holder_hits, axis=1)
    destination = holder * capacity + position
    places = pool_width * capacity
    hits = jnp.arange(places)[:, None] == destination[None, :]
    moving = hits.astype(bf16)
    send_tags = jnp.sum(jnp.where(hits, local_slot[None, :] + 1, 0), axis=1)

    width = features // CHUNKS
    received = []
    for chunk in range(CHUNKS):
        rows = jnp.dot(
            moving, tokens[:, chunk * width : (chunk + 1) * width], preferred_element_type=f32
        ).astype(bf16)
        received.append(exchange(rows.reshape(pool_width, capacity, width)).reshape(places, width))
    tags = exchange(send_tags.reshape(pool_width, capacity)).reshape(places)

    all_pos = lax.all_gather(tile_pos, "pool", axis=0, tiled=True)
    slot_hot = (slot[:, None] == jnp.arange(slot_total)[None, :])
    own_pos = [
        jnp.sum(jnp.where(slot_hot, all_pos[:, t][None, :], 0), axis=1) for t in range(per_shard)
    ]
    picks = []
    for t in range(per_shard):
        row_block = own_pos[t] // col_count
        picked = jnp.zeros((local_rows, tile_side), bf16)
        for block in range(features // tile_side):
            piece = tokens[:, block * tile_side : (block + 1) * tile_side]
            picked = jnp.where(row_block[:, None] == block, piece, picked)
        picks.append(picked)
    pick_rows = jnp.dot(
        moving, jnp.concatenate(picks, axis=1), preferred_element_type=f32
    ).astype(bf16)
    recv_picks = exchange(pick_rows.reshape(pool_width, capacity, -1)).reshape(places, -1)
    slot_mask = tags[:, None] == jnp.arange(1, slots_here + 1)[None, :]
    tile_mask = jnp.repeat(slot_mask, tile_side, axis=1)
    products = []
    for t in range(per_shard):
        feats = recv_picks[:, t * tile_side : (t + 1) * tile_side]
        spread = jnp.where(tile_mask, jnp.tile(feats, (1, slots_here)), jnp.zeros((), bf16))
        products.append(
            jnp.dot(
                spread, tile_data[:, t].reshape(-1, tile_side), preferred_element_type=f32
            )
        )
    home = exchange(jnp.concatenate(products, axis=1).reshape(pool_width, capacity, -1))
    own_products = jnp.take(home.reshape(places, -1), destination, axis=0)
    sparse = []
    for column in range(col_count):
        total = jnp.zeros((local_rows, tile_side), f32)
        for t in range(per_shard):
            col_block = own_pos[t] % col_count
            total = total + jnp.where(
                (col_block == column)[:, None],
                own_products[:, t * tile_side : (t + 1) * tile_side],
                0.0,
            )
        sparse.append(total)

    base = jnp.dot(
        lax.dynamic_slice_in_dim(tokens, group * share, share, axis=1),
        near_weight,
        preferred_element_type=f32,
    )
    far_weight = near_weight
    for step in range(1, group_width):
        ring = [(g, (g + 1) % group_width) for g in range(group_width)]
        far_weight = lax.ppermute(far_weight, "groups", ring)
        origin = lax.rem(group - step + group_width, group_width)
        base = base + jnp.dot(
            lax.dynamic_slice_in_dim(tokens, origin * share, share, axis=1),
            far_weight,
            preferred_element_type=f32,
        )
    summed = lax.psum_scatter(
        base + jnp.concatenate(sparse, axis=1), "tensor", scatter_dimension=1, tiled=True
    )

    own_b = lax.dynamic_slice_in_dim(
        low_b, lax.axis_index("tensor") * own_columns, own_columns, axis=1
    )
    all_b = lax.all_gather(own_b, "pool", axis=0, tiled=True)
    coeff = jnp.zeros((places, slots_here * RANK), f32)
    for chunk in range(CHUNKS):
        coeff = coeff + jnp.dot(
            received[chunk], low_a[chunk * width : (chunk + 1) * width], preferred_element_type=f32
        )
    coeff = jnp.where(jnp.repeat(slot_mask, RANK, axis=1), coeff, 0.0)
    fold = (jnp.arange(slots_here * RANK)[None, :] % RANK == jnp.arange(RANK)[:, None]).astype(f32)
    folded = lax.dot_general(
        fold, coeff, (((1,), (1,)), ((), ())), precision=lax.Precision.HIGHEST
    )
    folded = folded.reshape(RANK, pool_width, capacity).transpose(1, 0, 2)
    folded = jnp.broadcast_to(folded[:, None], (pool_width, tensor_width, RANK, capacity))
    returned = lax.all_to_all(
        folded.reshape(pool_width * tensor_width, RANK, capacity),
        ("pool", "tensor"),
        split_axis=0,
        concat_axis=0,
        tiled=True,
    )
    returned = jnp.sum(returned.reshape(pool_width, tensor_width, RANK, capacity), axis=1)
    returned = returned.transpose(0, 2, 1).reshape(places, RANK)
    own_coeff = lax.dot_general(
        hits.astype(f32), returned, (((0,), (0,)), ((), ())), precision=lax.Precision.HIGHEST
    )
    wide = jnp.where(
        jnp.repeat(slot_hot, RANK, axis=1), jnp.tile(own_coeff, (1, slot_total)), 0.0
    )
    low_rank = sum(jnp.dot(part, all_b, preferred_element_type=f32) for part in split3(wide))
    return (summed + low_rank).astype(bf16)


def solution(mesh):
    return jax.shard_map(
        local,
        mesh=mesh,
        in_specs=(
            P(("groups", "pool"), "tensor"),
            P(("groups", "pool")),
            P("groups"),
            P("tensor", "pool"),
            P("tensor", ("groups", "pool")),
            P(("groups", "pool"), None),
            P(("groups", "pool"), "tensor", None, None),
            P(("groups", "pool"), "tensor"),
        ),
        out_specs=P(("groups", "pool"), "tensor"),
        check_vma=False,
    )
```

time: 388 us -> 343 us (0.88)
  waiting for transfers between devices: 292 us -> 223 us
  local copies, waits for them, and re-layouts: 33.2 us -> 9.49 us
  other arithmetic: 4.42 us -> 23 us
  blocking collectives: 0 us -> 13.4 us
  starting transfers between devices: 15.4 us -> 26.1 us
  matrix products: 29.3 us -> 33.3 us
    all_to_all x3 -> x6, waiting for transfers between devices: 272 us -> 180 us  [the longest x5 175 us: exchange(): return lax.all_to_all(x, 'pool', split_axis=0, concat_axis=0, tiled=True)]
    ppermute x0 -> x1, waiting for transfers between devices: none -> 28.3 us  [local(): far_weight = lax.ppermute(far_weight, 'groups', ring)]
    all_gather x0 -> x1, blocking collectives: none -> 13.4 us  [local(): all_pos = lax.all_gather(tile_pos, 'pool', axis=0, tiled=True)]
    scatter x2 -> x0, local copies, waits for them, and re-layouts: 11.5 us -> none  [the longest x1 10.1 us: local(): jnp.zeros((pool_width * capacity, features), jnp.bfloat16).at[destination]]
    select_n x3 -> x7, other arithmetic: 0.04 us -> 10.6 us  [the longest x2 8.69 us: local(): picked = jnp.where(row_block[:, None] == block, piece, picked)]
    all_to_all x3 -> x6, starting transfers between devices: 15.2 us -> 24.3 us  [the longest x5 20.7 us: exchange(): return lax.all_to_all(x, 'pool', split_axis=0, concat_axis=0, tiled=True)]
    gather x2 -> x1, local copies, waits for them, and re-layouts: 7.94 us -> 0.97 us  [local(): own_products = jnp.take(home.reshape(places, -1), destination, axis=0)]
    unnamed x0 -> x7, other arithmetic: none -> 5.66 us
  transfers between devices with their start and end apart: 5 -> 10, of which waited for: 3 -> 7; matrix products, arithmetic and copies ran while one was open for 14% -> 18% of each run, Pallas kernels for 0% -> 0%
where the time goes in v1:
time: 343 us; the launch traced here: 342 us
  waiting for transfers between devices  223 us (65%)
  matrix products  33.3 us (10%)
  starting transfers between devices  26.1 us (8%)
  other arithmetic  23 us (7%)
  between operations  13.5 us (4%)
  blocking collectives  13.4 us (4%)
  local copies, waits for them, and re-layouts  9.49 us (3%)
    all_to_all x5, waiting for transfers between devices, exchange(): return lax.all_to_all(x, 'pool', split_axis=0, concat_axis=0, tiled=True)  175 us
    ppermute x1, waiting for transfers between devices, local(): far_weight = lax.ppermute(far_weight, 'groups', ring)  28.3 us
    all_to_all x5, starting transfers between devices, exchange(): return lax.all_to_all(x, 'pool', split_axis=0, concat_axis=0, tiled=True)  20.7 us
    reduce_scatter x1, waiting for transfers between devices, local(): lax.psum_scatter(base + jnp.concatenate(sparse, axis=1), 'tensor', scatte...  14.6 us
    all_gather x1, blocking collectives, local(): all_pos = lax.all_gather(tile_pos, 'pool', axis=0, tiled=True)  13.4 us
    select_n x2, other arithmetic, local(): picked = jnp.where(row_block[:, None] == block, piece, picked)  8.69 us
    dot_general x2, matrix products, local(): jnp.dot(moving, tokens[:, chunk * width:(chunk + 1) * width], preferred_e...  8.31 us
  transfers between devices with their start and end apart: 10, of which 7 were waited for; matrix products, arithmetic and copies ran while one was open for 18% of the time, Pallas kernels for 0%

profile of v1, /device:TPU:0, one launch (start us, length us, event | category | flops | bytes accessed | tf_op | source)
XLA Modules:
  0.0 342.3 jit_solution(4296011760250286088)
XLA Ops:
  6.6 1.4 copy-done
  7.9 0.9 constant_dynamic-slice_fusion.1
  9.0 13.4 %all-gather = s32[8,16,2]{1,2,0:T(2,128)S(1)} all-gather(s32[1,16,2]{1,2,0:T(2,128)S(1)} %bitcast.72), channel_id=1, replica_groups=mesh['groups'=2,'pool'=8,'tensor'=2] {'pool'}, dimensions={0}, use_global_device_ids=true | all-gather | bytes 1152 | tf_op jit(solution)/shard_map/all_gather | solution.py:65
  23.8 3.3 all-to-all-start
  27.2 6.1 %select_select_fusion = bf16[256,128]{1,0:T(8,128)(2,1)S(1)} fusion(pred[256]{0:T(512)(128)(4,1)S(1)} %get-tuple-element.142, pred[256]{0:T(512)(128)(4,1)S(1)} %get-tuple-element.187, pred[256]{0:T(512)(128)(4,1)S(1)} %get-tuple-element.186, pred[256]{0:T(512)(128)(4,1)S(1)} %get-tuple-element.185, pred[256]{0:T(512)(128)(4,1)S(1)} %get-tuple-element.184, ...), kind=kLoop, calls=%fused_computation.66 | loop fusion | flops 1572864 | bytes 3223552 | tf_op jit(solution)/shard_map/jit(_where)/select_n | solution.py:76
  33.3 2.6 select_select_fusion.1
  35.9 0.9 convolution_convert_fusion.2
  36.9 4.9 %all-to-all-start.1 = ((bf16[8,64,256]{2,1,0:T(8,128)(2,1)}), bf16[8,64,256]{2,1,0:T(8,128)(2,1)S(1)}, u32[]{:S(2)}, u32[]{:S(2)}) async-start(bf16[8,64,256]{2,1,0:T(8,128)(2,1)} %bitcast.3), calls=%async_computation.1 | async-start | bytes 524288 | tf_op jit(solution)/shard_map/all_to_all | solution.py:35
  44.3 13.8 %all-to-all-done.1 = bf16[8,64,256]{2,1,0:T(8,128)(2,1)S(1)} async-done(((bf16[8,64,256]{2,1,0:T(8,128)(2,1)}), bf16[8,64,256]{2,1,0:T(8,128)(2,1)S(1)}, u32[]{:S(2)}, u32[]{:S(2)}) %all-to-all-start.1) | async-done | bytes 262176 | tf_op jit(solution)/shard_map/all_to_all | solution.py:35
  58.2 1.4 broadcast_select_fusion.1
  61.3 1.0 copy.23
  62.3 3.5 %all-to-all-start.2 = ((f32[8,64,256]{2,1,0:T(8,128)}), f32[8,64,256]{2,1,0:T(8,128)S(1)}, u32[]{:S(2)}, u32[]{:S(2)}) async-start(f32[8,64,256]{2,1,0:T(8,128)} %bitcast.7), calls=%async_computation.2 | async-start | bytes 1048576 | tf_op jit(solution)/shard_map/all_to_all | solution.py:35
  65.8 4.1 %convolution_convert_fusion = bf16[512,3072]{1,0:T(8,128)(2,1)} fusion(bf16[256,6144]{1,0:T(8,128)(2,1)} %param.8, s32[256]{0:T(256)S(1)} %get-tuple-element.12), kind=kOutput, calls=%fused_computation.1 | convolution fusion | flops 807010304 | bytes 4719616 | tf_op jit(solution)/shard_map/dot_general | solution.py:59
  69.9 17.7 %all-to-all-done.2 = f32[8,64,256]{2,1,0:T(8,128)S(1)} async-done(((f32[8,64,256]{2,1,0:T(8,128)}), f32[8,64,256]{2,1,0:T(8,128)S(1)}, u32[]{:S(2)}, u32[]{:S(2)}) %all-to-all-start.2) | async-done | bytes 524320 | tf_op jit(solution)/shard_map/all_to_all | solution.py:35
  87.7 4.5 %all-to-all-start.4 = ((bf16[8,64,3072]{2,1,0:T(8,128)(2,1)}), bf16[8,64,3072]{2,1,0:T(8,128)(2,1)}, u32[]{:S(2)}, u32[]{:S(2)}) async-start(bf16[8,64,3072]{2,1,0:T(8,128)(2,1)} %bitcast.58), calls=%async_computation.5 | async-start | bytes 6291456 | tf_op jit(solution)/shard_map/all_to_all | solution.py:35
  92.2 4.2 %convolution_convert_fusion.1 = bf16[512,3072]{1,0:T(8,128)(2,1)} fusion(bf16[256,6144]{1,0:T(8,128)(2,1)} %param.8, s32[256]{0:T(256)S(1)} %get-tuple-element.12), kind=kOutput, calls=%fused_computation.2 | convolution fusion | flops 807010304 | bytes 4719616 | tf_op jit(solution)/shard_map/dot_general | solution.py:59
  96.4 67.3 %all-to-all-done.4 = bf16[8,64,3072]{2,1,0:T(8,128)(2,1)} async-done(((bf16[8,64,3072]{2,1,0:T(8,128)(2,1)}), bf16[8,64,3072]{2,1,0:T(8,128)(2,1)}, u32[]{:S(2)}, u32[]{:S(2)}) %all-to-all-start.4) | async-done | bytes 3145760 | tf_op jit(solution)/shard_map/all_to_all | solution.py:35
  163.7 4.6 %all-to-all-start.3 = ((bf16[8,64,3072]{2,1,0:T(8,128)(2,1)}), bf16[8,64,3072]{2,1,0:T(8,128)(2,1)}, u32[]{:S(2)}, u32[]{:S(2)}) async-start(bf16[8,64,3072]{2,1,0:T(8,128)(2,1)} %bitcast.57), calls=%async_computation.4 | async-start | bytes 6291456 | tf_op jit(solution)/shard_map/all_to_all | solution.py:35
  168.4 1.5 collective-permute-start
  171.0 1.0 gather_fusion
  177.8 3.0 fusion.7
  180.8 75.9 %all-to-all-done.3 = bf16[8,64,3072]{2,1,0:T(8,128)(2,1)} async-done(((bf16[8,64,3072]{2,1,0:T(8,128)(2,1)}), bf16[8,64,3072]{2,1,0:T(8,128)(2,1)}, u32[]{:S(2)}, u32[]{:S(2)}) %all-to-all-start.3) | async-done | bytes 3145760 | tf_op jit(solution)/shard_map/all_to_all | solution.py:35
  256.7 3.3 fusion.26
  261.2 3.5 %all-to-all-start.5 = ((f32[16,1,1024]{2,1,0:T(1,128)}), f32[16,1,1024]{2,1,0:T(1,128)S(1)}, u32[]{:S(2)}, u32[]{:S(2)}) async-start(f32[16,1,1024]{2,1,0:T(1,128)} %reshape.736), calls=%async_computation.6 | async-start | bytes 131072 | tf_op jit(solution)/shard_map/all_to_all | solution.py:142
  265.8 5.6 %all-to-all-done.5 = f32[16,1,1024]{2,1,0:T(1,128)S(1)} async-done(((f32[16,1,1024]{2,1,0:T(1,128)}), f32[16,1,1024]{2,1,0:T(1,128)S(1)}, u32[]{:S(2)}, u32[]{:S(2)}) %all-to-all-start.5) | async-done | bytes 65568 | tf_op jit(solution)/shard_map/all_to_all | solution.py:142
  273.0 5.2 %fusion.15 = f32[256,1024]{1,0:T(8,128)S(1)} fusion(bf16[3072,1024]{1,0:T(8,128)(2,1)} %all-gather.4.cloned.1.call-done, bf16[256,6144]{1,0:T(8,128)(2,1)} %param.8, s32[]{:T(128)S(6)} %select_n.844), kind=kOutput, calls=%fused_computation.24 | convolution fusion | flops 1610612736 | bytes 8912900 | tf_op jit(solution)/shard_map/dot_general | solution.py:107
  278.2 28.3 %collective-permute-done = bf16[3072,1024]{1,0:T(8,128)(2,1)} collective-permute-done((bf16[3072,1024]{1,0:T(8,128)(2,1)}, bf16[3072,1024]{1,0:T(8,128)(2,1)}, u32[]{:S(2)}, u32[]{:S(2)}) %collective-permute-start) | collective-permute-done | bytes 6291488 | tf_op jit(solution)/shard_map/ppermute | solution.py:115
  306.5 5.9 %fusion.20 = f32[256,1024]{1,0:T(8,128)} fusion(f32[256,1024]{1,0:T(8,128)} %add_dynamic-update-slice_fusion, f32[256,1024]{1,0:T(8,128)S(1)} %fusion.15, bf16[3072,1024]{1,0:T(8,128)(2,1)} %collective-permute-done, bf16[256,6144]{1,0:T(8,128)(2,1)S(1)} %copy-done.2, s32[]{:T(128)S(6)} %select_n.845), kind=kOutput, calls=%fused_computation.27 | convolution fusion | flops 1611137024 | bytes 11010052 | tf_op jit(solution)/shard_map/dot_general | solution.py:117
  313.1 1.9 fusion
  315.0 2.8 fusion.49
  319.4 14.6 %reduce-scatter.2.cloned.1.call-done = f32[256,512]{1,0:T(8,128)} async-done(((f32[256,1024]{1,0:T(8,128)}), f32[256,512]{1,0:T(8,128)}) %reduce-scatter.2.cloned.1.call-update) | async-done | bytes 524304 | tf_op jit(solution)/shard_map/reduce_scatter | solution.py:122
  333.9 1.8 add_convert_fusion
  (88 shorter events, 18.7 us)
Async XLA Ops:
  6.5 1.4 copy-start
  6.5 2.4 copy-start.9
  6.5 2.4 copy-start.8
  6.5 2.5 copy-start.7
  6.5 161.8 %all-gather.4.cloned.1.call-start = ((), (), s32[]{:S(2)}) async-start(), calls=%async_computation.7 | async-start | bytes 7077888 | tf_op jit(solution)/shard_map/all_gather | solution.py:40
  23.8 13.1 %all-to-all-start = ((s32[8,1,64]{2,1,0:T(1,128)}), s32[8,1,64]{2,1,0:T(1,128)S(1)}, u32[]{:S(2)}, u32[]{:S(2)}) async-start(s32[8,1,64]{2,1,0:T(1,128)} %all_to_all.21), calls=%async_computation | async-start | bytes 8192 | tf_op jit(solution)/shard_map/all_to_all | solution.py:35
  27.1 6.2 %copy-start.1 = (bf16[256,6144]{1,0:T(8,128)(2,1)S(1)}, bf16[256,6144]{1,0:T(8,128)(2,1)}, u32[]{:S(2)}) copy-start(bf16[256,6144]{1,0:T(8,128)(2,1)} %param.8) | copy-start | bytes 9437188
  33.3 8.5 %copy-start.4 = (bf16[16,2,128,128]{3,2,1,0:T(8,128)(2,1)S(1)}, bf16[16,2,128,128]{3,2,1,0:T(8,128)(2,1)}, u32[]{:S(2)}) copy-start(bf16[16,2,128,128]{3,2,1,0:T(8,128)(2,1)} %param.14) | copy-start | bytes 3145732
  36.9 21.3 %all-to-all-start.1 = ((bf16[8,64,256]{2,1,0:T(8,128)(2,1)}), bf16[8,64,256]{2,1,0:T(8,128)(2,1)S(1)}, u32[]{:S(2)}, u32[]{:S(2)}) async-start(bf16[8,64,256]{2,1,0:T(8,128)(2,1)} %bitcast.3), calls=%async_computation.1 | async-start | bytes 524288 | tf_op jit(solution)/shard_map/all_to_all | solution.py:35
  58.2 1.4 copy-start.5
  62.3 25.3 %all-to-all-start.2 = ((f32[8,64,256]{2,1,0:T(8,128)}), f32[8,64,256]{2,1,0:T(8,128)S(1)}, u32[]{:S(2)}, u32[]{:S(2)}) async-start(f32[8,64,256]{2,1,0:T(8,128)} %bitcast.7), calls=%async_computation.2 | async-start | bytes 1048576 | tf_op jit(solution)/shard_map/all_to_all | solution.py:35
  87.7 76.0 %all-to-all-start.4 = ((bf16[8,64,3072]{2,1,0:T(8,128)(2,1)}), bf16[8,64,3072]{2,1,0:T(8,128)(2,1)}, u32[]{:S(2)}, u32[]{:S(2)}) async-start(bf16[8,64,3072]{2,1,0:T(8,128)(2,1)} %bitcast.58), calls=%async_computation.5 | async-start | bytes 6291456 | tf_op jit(solution)/shard_map/all_to_all | solution.py:35
  163.7 6.2 %copy-start.6 = (bf16[256,1024]{1,0:T(8,128)(2,1)S(1)}, bf16[256,1024]{1,0:T(8,128)(2,1)}, u32[]{:S(2)}) copy-start(bf16[256,1024]{1,0:T(8,128)(2,1)} %param.13) | copy-start | bytes 1572868
  163.7 93.0 %all-to-all-start.3 = ((bf16[8,64,3072]{2,1,0:T(8,128)(2,1)}), bf16[8,64,3072]{2,1,0:T(8,128)(2,1)}, u32[]{:S(2)}, u32[]{:S(2)}) async-start(bf16[8,64,3072]{2,1,0:T(8,128)(2,1)} %bitcast.57), calls=%async_computation.4 | async-start | bytes 6291456 | tf_op jit(solution)/shard_map/all_to_all | solution.py:35
  168.3 146.7 %all-gather.6.cloned.1.call-start = ((), (), s32[]{:S(2)}) async-start(), calls=%async_computation.9 | async-start | bytes 2359296 | tf_op jit(solution)/shard_map/all_gather | solution.py:129
  168.4 138.1 %collective-permute-start = (bf16[3072,1024]{1,0:T(8,128)(2,1)}, bf16[3072,1024]{1,0:T(8,128)(2,1)}, u32[]{:S(2)}, u32[]{:S(2)}) collective-permute-start(bf16[3072,1024]{1,0:T(8,128)(2,1)} %all-gather.4.cloned.1.call-done), channel_id=1, source_target_pairs={{0,16},{16,0},{1,17},{17,1},{2,18},{18,2},{3,19},{19,3},{4,20},{20... | collective-permute-start | bytes 18874376 | tf_op jit(solution)/shard_map/ppermute | solution.py:115
  172.0 5.8 %copy-start.10 = (bf16[6144,256]{1,0:T(8,128)(2,1)S(1)}, bf16[6144,256]{1,0:T(8,128)(2,1)}, u32[]{:S(2)}) copy-start(bf16[6144,256]{1,0:T(8,128)(2,1)} %param.12) | copy-start | bytes 9437188
  261.2 10.2 %all-to-all-start.5 = ((f32[16,1,1024]{2,1,0:T(1,128)}), f32[16,1,1024]{2,1,0:T(1,128)S(1)}, u32[]{:S(2)}, u32[]{:S(2)}) async-start(f32[16,1,1024]{2,1,0:T(1,128)} %reshape.736), calls=%async_computation.6 | async-start | bytes 131072 | tf_op jit(solution)/shard_map/all_to_all | solution.py:142
  264.8 69.2 %reduce-scatter.2.cloned.1.call-start = ((), (), s32[]{:S(2)}) async-start(), calls=%async_computation.8 | async-start | bytes 1572864 | tf_op jit(solution)/shard_map/reduce_scatter | solution.py:122
  273.0 33.5 %copy-start.2 = (bf16[256,6144]{1,0:T(8,128)(2,1)S(1)}, bf16[256,6144]{1,0:T(8,128)(2,1)}, u32[]{:S(2)}) copy-start(bf16[256,6144]{1,0:T(8,128)(2,1)} %param.8) | copy-start | bytes 9437188
  315.0 2.8 copy-start.3
  315.0 2.9 copy-start.11
Sparse Core Ops, SparseCore 0:
  9.0 85.2 all-gather.3
  170.8 49.3 all-gather.5
  312.5 21.3 reduce-scatter.1

commit v2 on v0

v2 whole, which is shorter than its diff:
```python
import jax
import jax.numpy as jnp
from jax import lax
from jax.sharding import PartitionSpec as P

RANK = 16
CHUNKS = 3
BF16 = jnp.bfloat16
F32 = jnp.float32


def split3(x):
    high = lax.reduce_precision(x, 8, 7)
    rest = x - high
    mid = lax.reduce_precision(rest, 8, 7)
    low = rest - mid
    return [part.astype(BF16) for part in (high, mid, low)]


def dot(a, b):
    return jnp.dot(a, b, preferred_element_type=F32)


def exchange(x):
    return lax.all_to_all(x, "pool", split_axis=0, concat_axis=0, tiled=True)


def after(x, *others):
    for other in others:
        x = x + (lax.slice(other, (0,) * other.ndim, (1,) * other.ndim).reshape((1,) * x.ndim) * 0).astype(x.dtype)
    return x


def local(tokens, tenant_ids, slot_table, value_weight, low_a, low_b, tile_data, tile_pos):
    local_rows, features = tokens.shape
    pool_width = lax.axis_size("pool")
    tensor_width = lax.axis_size("tensor")
    group_width = lax.axis_size("groups")
    me = lax.axis_index("pool")
    group = lax.axis_index("groups")
    slots_here = low_b.shape[0] // RANK
    columns = low_b.shape[1]
    own_columns = columns // tensor_width
    tile_side = tile_data.shape[-1]
    per_shard = tile_pos.shape[1]
    col_count = columns // tile_side
    slot_total = slot_table.shape[0]
    capacity = 2 * local_rows // pool_width
    main_cap = capacity * 5 // 8
    extra_cap = capacity // 2
    left_cap = capacity - main_cap
    mains = pool_width * main_cap
    extras = pool_width * extra_cap
    lefts = pool_width * left_cap

    match_table = tenant_ids[:, None] == jnp.arange(slot_total)[None, :]
    slot = jnp.sum(jnp.where(match_table, slot_table[None, :], 0), axis=1)
    holder = slot // slots_here
    holder_hits = (holder[:, None] == jnp.arange(pool_width)[None, :]).astype(jnp.int32)
    earlier = (jnp.arange(local_rows)[:, None] >= jnp.arange(local_rows)[None, :]).astype(BF16)
    ranks = dot(earlier, holder_hits.astype(BF16)).astype(jnp.int32)
    position = jnp.sum((ranks - 1) * holder_hits, axis=1)
    over = position >= main_cap
    over_rank = jnp.sum(
        jnp.where(
            (jnp.arange(local_rows)[:, None] > jnp.arange(local_rows)[None, :]) & over[None, :], 1, 0
        ),
        axis=1,
    )
    left = over & (over_rank >= extra_cap)
    main_place = jnp.where(over, -1, holder * main_cap + position)
    extra_place = jnp.where(over & ~left, over_rank, -1)
    left_place = jnp.where(left, holder * left_cap + position - main_cap, -1)
    main_hits = jnp.arange(mains)[:, None] == main_place[None, :]
    extra_hits = jnp.arange(extra_cap)[:, None] == extra_place[None, :]

    def tags_of(hits):
        return jnp.sum(jnp.where(hits, slot[None, :] + 1, 0), axis=1)

    def mask_of(tags):
        return (tags - 1 - me * slots_here)[:, None] == jnp.arange(slots_here)[None, :]

    ints = jnp.concatenate(
        [
            tags_of(main_hits),
            tags_of(extra_hits),
            tile_pos.reshape(-1),
            jnp.sum(left.astype(jnp.int32))[None],
        ]
    )
    every = lax.all_gather(ints, ("groups", "pool"), axis=0)
    any_left = jnp.sum(every[:, -1]) > 0
    mine = lax.dynamic_slice_in_dim(every, group * pool_width, pool_width, axis=0)
    main_tags = lax.dynamic_slice_in_dim(mine, me * main_cap, main_cap, axis=1).reshape(-1)
    extra_tags = mine[:, mains : mains + extra_cap].reshape(-1)
    all_pos = mine[:, mains + extra_cap : -1].reshape(slot_total, per_shard)
    main_mask = mask_of(main_tags)
    extra_mask = mask_of(extra_tags)

    share = features // group_width
    part_weight = lax.dynamic_slice_in_dim(value_weight, group * share, share, axis=0)
    near_weight = lax.all_gather(part_weight, "pool", axis=1, tiled=True)

    moving = main_hits.astype(BF16)
    width = features // CHUNKS

    def rows_of(chunk):
        rows = dot(moving, tokens[:, chunk * width : (chunk + 1) * width]).astype(BF16)
        return rows.reshape(pool_width, main_cap, width)

    received = [exchange(rows_of(0))]

    slot_hot = slot[:, None] == jnp.arange(slot_total)[None, :]
    own_pos = [
        jnp.sum(jnp.where(slot_hot, all_pos[:, t][None, :], 0), axis=1) for t in range(per_shard)
    ]
    picks = []
    for t in range(per_shard):
        row_block = own_pos[t] // col_count
        picked = jnp.zeros((local_rows, tile_side), BF16)
        for block in range(features // tile_side):
            piece = tokens[:, block * tile_side : (block + 1) * tile_side]
            picked = jnp.where(row_block[:, None] == block, piece, picked)
        picks.append(picked)
    picks = jnp.concatenate(picks, axis=1)
    extra_moving = extra_hits.astype(BF16)
    extra_rows = jnp.concatenate(
        [dot(extra_moving, tokens).astype(BF16), dot(extra_moving, picks).astype(BF16)], axis=1
    )
    extra_rows = lax.all_gather(extra_rows, "pool", axis=0, tiled=True)
    pick_rows = dot(moving, picks).astype(BF16).reshape(pool_width, main_cap, -1)
    main_picks = exchange(after(pick_rows, received[0])).reshape(mains, -1)

    received.append(exchange(after(rows_of(1), main_picks, near_weight)))

    base = dot(lax.dynamic_slice_in_dim(tokens, group * share, share, axis=1), near_weight)
    core = lax.rem(me, 2)
    half = columns // 2
    quarter = half // 2
    swap = [(p, p ^ 1) for p in range(pool_width)]
    first_pieces = []
    pieces = [
        lax.dynamic_slice_in_dim(near_weight, core * half + q * quarter, quarter, axis=1)
        for q in range(2)
    ]
    for step in range(1, group_width):
        ring = [(g, (g + 1) % group_width) for g in range(group_width)]
        origin = lax.rem(group - step + group_width, group_width)
        feats = lax.dynamic_slice_in_dim(tokens, origin * share, share, axis=1)
        pieces = [lax.ppermute(piece, "groups", ring) for piece in pieces]
        first_pieces.append(pieces[0])
        others = [lax.ppermute(piece, "pool", swap) for piece in pieces]
        own = [dot(feats, piece) for piece in pieces]
        far = [dot(feats, piece) for piece in others]
        base = base + jnp.where(
            core == 0,
            jnp.concatenate(own + far, axis=1),
            jnp.concatenate(far + own, axis=1),
        )

    def tile_products(feats, mask):
        tile_mask = jnp.repeat(mask, tile_side, axis=1)
        products = []
        for t in range(per_shard):
            wide = jnp.tile(feats[:, t * tile_side : (t + 1) * tile_side], (1, slots_here))
            wide = jnp.where(tile_mask, wide, jnp.zeros((), BF16))
            products.append(dot(wide, tile_data[:, t].reshape(-1, tile_side)))
        return jnp.concatenate(products, axis=1)

    fold = (jnp.arange(slots_here * RANK)[None, :] % RANK == jnp.arange(RANK)[:, None]).astype(F32)

    def folded(coeff, mask):
        coeff = jnp.where(jnp.repeat(mask, RANK, axis=1), coeff, 0.0)
        return lax.dot_general(
            fold, coeff, (((1,), (1,)), ((), ())), precision=lax.Precision.HIGHEST
        )

    def pick_back(hits, x):
        return lax.dot_general(
            hits.astype(F32), x, (((0,), (0,)), ((), ())), precision=lax.Precision.HIGHEST
        )

    products = jnp.concatenate(
        [
            tile_products(main_picks, main_mask).reshape(pool_width, main_cap, -1),
            tile_products(extra_rows[:, features:], extra_mask).reshape(pool_width, extra_cap, -1),
        ],
        axis=1,
    )
    home = exchange(after(products, received[1], *first_pieces))
    for chunk in range(2, CHUNKS):
        received.append(exchange(after(rows_of(chunk), home)))
    back_hits = jnp.concatenate([main_hits, extra_hits], axis=0)
    own_products = pick_back(
        back_hits,
        jnp.concatenate(
            [home[:, :main_cap].reshape(mains, -1), jnp.sum(home[:, main_cap:], axis=0)], axis=0
        ),
    )

    main_coeff = jnp.zeros((mains, slots_here * RANK), F32)
    for chunk in range(CHUNKS):
        main_coeff = main_coeff + dot(
            received[chunk].reshape(mains, width), low_a[chunk * width : (chunk + 1) * width]
        )
    extra_coeff = dot(extra_rows[:, :features], low_a)
    sent = jnp.concatenate(
        [
            folded(main_coeff, main_mask).reshape(RANK, pool_width, main_cap),
            folded(extra_coeff, extra_mask).reshape(RANK, pool_width, extra_cap),
        ],
        axis=2,
    )

    def coeff_back(x):
        x = jnp.broadcast_to(
            x.transpose(1, 0, 2)[:, None], (pool_width, tensor_width, RANK, x.shape[2])
        )
        x = lax.all_to_all(
            x.reshape(pool_width * tensor_width, RANK, -1),
            ("pool", "tensor"),
            split_axis=0,
            concat_axis=0,
            tiled=True,
        )
        x = jnp.sum(x.reshape(pool_width, tensor_width, RANK, -1), axis=1)
        return x.transpose(0, 2, 1)

    coeffs = coeff_back(sent)
    own_coeff = pick_back(
        back_hits,
        jnp.concatenate(
            [coeffs[:, :main_cap].reshape(mains, RANK), jnp.sum(coeffs[:, main_cap:], axis=0)],
            axis=0,
        ),
    )

    def leftover():
        hits = jnp.arange(lefts)[:, None] == left_place[None, :]
        chosen = hits.astype(BF16)
        rows = jnp.concatenate([dot(chosen, tokens), dot(chosen, picks)], axis=1).astype(BF16)
        rows = exchange(rows.reshape(pool_width, left_cap, -1)).reshape(lefts, -1)
        tags = exchange(tags_of(hits).reshape(pool_width, left_cap)).reshape(lefts)
        mask = mask_of(tags)
        tiles = tile_products(rows[:, features:], mask)
        tiles = exchange(tiles.reshape(pool_width, left_cap, -1)).reshape(lefts, -1)
        part = folded(dot(rows[:, :features], low_a), mask)
        part = coeff_back(part.reshape(RANK, pool_width, left_cap)).reshape(lefts, RANK)
        return pick_back(hits, tiles), pick_back(hits, part)

    def nothing():
        return (
            jnp.zeros((local_rows, per_shard * tile_side), F32),
            jnp.zeros((local_rows, RANK), F32),
        )

    more_products, more_coeff = lax.cond(any_left, leftover, nothing)
    own_products = own_products + more_products
    own_coeff = own_coeff + more_coeff

    sparse = []
    for column in range(col_count):
        total = jnp.zeros((local_rows, tile_side), F32)
        for t in range(per_shard):
            total = total + jnp.where(
                (own_pos[t] % col_count == column)[:, None],
                own_products[:, t * tile_side : (t + 1) * tile_side],
                0.0,
            )
        sparse.append(total)
    summed = lax.psum_scatter(
        base + jnp.concatenate(sparse, axis=1), "tensor", scatter_dimension=1, tiled=True
    )

    own_b = lax.dynamic_slice_in_dim(
        low_b, lax.axis_index("tensor") * own_columns, own_columns, axis=1
    )
    all_b = lax.all_gather(own_b, "pool", axis=0, tiled=True)
    wide = jnp.where(
        jnp.repeat(slot_hot, RANK, axis=1), jnp.tile(own_coeff, (1, slot_total)), 0.0
    )
    low_rank = sum(dot(part, all_b) for part in split3(wide))
    return (summed + low_rank).astype(BF16)


def solution(mesh):
    return jax.shard_map(
        local,
        mesh=mesh,
        in_specs=(
            P(("groups", "pool"), "tensor"),
            P(("groups", "pool")),
            P("groups"),
            P("tensor", "pool"),
            P("tensor", ("groups", "pool")),
            P(("groups", "pool"), None),
            P(("groups", "pool"), "tensor", None, None),
            P(("groups", "pool"), "tensor"),
        ),
        out_specs=P(("groups", "pool"), "tensor"),
        check_vma=False,
    )
```

time: 388 us -> 365 us (0.941)
  waiting for transfers between devices: 292 us -> 145 us
  blocking collectives: 0 us -> 64.8 us
  other arithmetic: 4.42 us -> 30 us
  matrix products: 29.3 us -> 47.6 us
  starting transfers between devices: 15.4 us -> 27.5 us
  between operations: 13.6 us -> 19.5 us
  local copies, waits for them, and re-layouts: 33.2 us -> 28.1 us
    all_to_all x3 -> x6, waiting for transfers between devices: 272 us -> 87.2 us  [the longest x5 79.8 us: exchange(): return lax.all_to_all(x, 'pool', split_axis=0, concat_axis=0, tiled=True)]
    unnamed x0 -> x1, blocking collectives: none -> 64.8 us
    ppermute x0 -> x4, waiting for transfers between devices: none -> 58 us  [the longest x2 58 us: local(): pieces = [lax.ppermute(piece, 'groups', ring) for piece in pieces]]
    reduce_scatter x1, waiting for transfers between devices: 19.3 us -> 0.02 us  [local(): lax.psum_scatter(base + jnp.concatenate(sparse, axis=1), 'tensor', scatte...]
    dot_general x5 -> x27, matrix products: 29.3 us -> 47.6 us  [the longest x23 45 us: dot(): return jnp.dot(a, b, preferred_element_type=F32)]
    select_n x4 -> x8, other arithmetic: 0.05 us -> 13.4 us  [the longest x2 8.48 us: local(): picked = jnp.where(row_block[:, None] == block, piece, picked)]
    scatter x2 -> x0, local copies, waits for them, and re-layouts: 11.5 us -> none  [the longest x1 10.1 us: local(): jnp.zeros((pool_width * capacity, features), jnp.bfloat16).at[destination]]
    slice x1 -> x12, local copies, waits for them, and re-layouts: 0.21 us -> 11.3 us  [the longest x6 6.75 us: after(): lax.slice(other, (0,) * other.ndim, (1,) * other.ndim)]
  transfers between devices with their start and end apart: 5 -> 14, of which waited for: 3 -> 7; matrix products, arithmetic and copies ran while one was open for 14% -> 27% of each run, Pallas kernels for 0% -> 0%
where the time goes in v2:
time: 365 us; the launch traced here: 363 us
  waiting for transfers between devices  145 us (40%)
  blocking collectives  64.8 us (18%)
  matrix products  47.6 us (13%)
  other arithmetic  30 us (8%)
  local copies, waits for them, and re-layouts  28.1 us (8%)
  starting transfers between devices  27.5 us (8%)
  between operations  19.5 us (5%)
    all_to_all x5, waiting for transfers between devices, exchange(): return lax.all_to_all(x, 'pool', split_axis=0, concat_axis=0, tiled=True)  79.8 us
    unnamed x1, blocking collectives  64.8 us
    ppermute x2, waiting for transfers between devices, local(): pieces = [lax.ppermute(piece, 'groups', ring) for piece in pieces]  58 us
    dot_general x23, matrix products, dot(): return jnp.dot(a, b, preferred_element_type=F32)  45 us
    all_to_all x5, starting transfers between devices, exchange(): return lax.all_to_all(x, 'pool', split_axis=0, concat_axis=0, tiled=True)  21.5 us
    select_n x2, other arithmetic, local(): picked = jnp.where(row_block[:, None] == block, piece, picked)  8.48 us
    all_to_all x1, waiting for transfers between devices, coeff_back(): lax.all_to_all(x.reshape(pool_width * tensor_width, RANK, -1), ('pool', '...  7.44 us
  transfers between devices with their start and end apart: 14, of which 7 were waited for; matrix products, arithmetic and copies ran while one was open for 27% of the time, Pallas kernels for 0%

profile of v2, /device:TPU:0, one launch (start us, length us, event | category | flops | bytes accessed | tf_op | source)
XLA Modules:
  0.0 363.0 jit_solution(713926856706832793)
XLA Ops:
  13.4 64.8 %all-reduce = s32[6160]{0:T(1024)S(1)} all-reduce(s32[6160]{0:T(1024)S(1)} %add_dynamic-update-slice_fusion.8), channel_id=2, replica_groups=mesh['groups'=2,'pool'=8,'tensor'=2] {'groups','pool'}, use_global_device_ids=true, to_apply=%add | all-reduce | flops 6160 | bytes 49280
  80.7 5.9 %select_select_fusion = bf16[256,128]{1,0:T(8,128)(2,1)S(1)} fusion(pred[256]{0:T(512)(128)(4,1)S(1)} %get-tuple-element.225, pred[256]{0:T(512)(128)(4,1)S(1)} %get-tuple-element.180, pred[256]{0:T(512)(128)(4,1)S(1)} %get-tuple-element.181, pred[256]{0:T(512)(128)(4,1)S(1)} %get-tuple-element.182, pred[256]{0:T(512)(128)(4,1)S(1)} %get-tuple-element.183, ...), kind=kLoop, calls=%fused_computation.138 | loop fusion | flops 1572864 | bytes 3223552 | tf_op jit(solution)/shard_map/jit(_where)/select_n | solution.py:123
  86.7 2.6 select_select_fusion.1
  93.4 2.3 convolution_convert_fusion.5
  95.7 4.3 %all-to-all-start.4 = ((bf16[8,40,2048]{2,1,0:T(8,128)(2,1)}), bf16[8,40,2048]{2,1,0:T(8,128)(2,1)}, u32[]{:S(2)}, u32[]{:S(2)}) async-start(bf16[8,40,2048]{2,1,0:T(8,128)(2,1)} %bitcast.114), calls=%async_computation.4 | async-start | bytes 2621440 | tf_op jit(solution)/shard_map/all_to_all | solution.py:25
  106.6 2.4 fusion.100
  108.9 45.4 %all-to-all-done.4 = bf16[8,40,2048]{2,1,0:T(8,128)(2,1)} async-done(((bf16[8,40,2048]{2,1,0:T(8,128)(2,1)}), bf16[8,40,2048]{2,1,0:T(8,128)(2,1)}, u32[]{:S(2)}, u32[]{:S(2)}) %all-to-all-start.4) | async-done | bytes 1310752 | tf_op jit(solution)/shard_map/all_to_all | solution.py:25
  157.1 3.6 all-to-all-start.5
  160.7 2.9 fusion.52
  163.6 8.2 %all-to-all-done.5 = bf16[8,40,256]{2,1,0:T(8,128)(2,1)S(1)} async-done(((bf16[8,40,256]{2,1,0:T(8,128)(2,1)}), bf16[8,40,256]{2,1,0:T(8,128)(2,1)S(1)}, u32[]{:S(2)}, u32[]{:S(2)}) %all-to-all-start.5) | async-done | bytes 163872 | tf_op jit(solution)/shard_map/all_to_all | solution.py:25
  173.1 2.2 broadcast_select_fusion.3
  179.9 4.3 %all-to-all-start.6 = ((bf16[8,40,2048]{2,1,0:T(8,128)(2,1)}), bf16[8,40,2048]{2,1,0:T(8,128)(2,1)}, u32[]{:S(2)}, u32[]{:S(2)}) async-start(bf16[8,40,2048]{2,1,0:T(8,128)(2,1)} %bitcast.115), calls=%async_computation.6 | async-start | bytes 2621440 | tf_op jit(solution)/shard_map/all_to_all | solution.py:25
  184.2 3.9 %constant_dynamic-slice_fusion.1 = (bf16[3072,256]{1,0:T(8,128)(2,1)}, bf16[3072,256]{1,0:T(8,128)(2,1)}) fusion(bf16[3072,1024]{1,0:T(8,128)(2,1)} %all-gather.5.cloned.1.call-done, s32[]{:T(128)S(6)} %select_n.932, s32[]{:T(128)S(6)} %select_n.931), kind=kLoop, calls=%fused_computation.184 | loop fusion | bytes 6291464 | tf_op jit(solution)/shard_map/dynamic_slice | solution.py:143
  190.8 3.8 %fusion.35 = f32[256,256]{1,0:T(8,128)S(1)} fusion(pred[256,256]{1,0:T(32,128)(4,1)} %copy.76, bf16[6144,256]{1,0:T(8,128)(2,1)} %param.14, bf16[256,6400]{1,0:T(8,128)(2,1)} %all-gather.7.cloned.1.call-done), kind=kOutput, calls=%fused_computation.65 | convolution fusion | flops 805371904 | bytes 6619136 | tf_op jit(solution)/shard_map/dot_general | solution.py:21
  197.9 2.4 broadcast_select_fusion.6
  200.3 25.4 %collective-permute-done.1 = bf16[3072,256]{1,0:T(8,128)(2,1)} collective-permute-done((bf16[3072,256]{1,0:T(8,128)(2,1)}, bf16[3072,256]{1,0:T(8,128)(2,1)}, u32[]{:S(2)}, u32[]{:S(2)}) %collective-permute-start.1) | collective-permute-done | bytes 1572896 | tf_op jit(solution)/shard_map/ppermute | solution.py:150
  226.1 32.6 %collective-permute-done = bf16[3072,256]{1,0:T(8,128)(2,1)} collective-permute-done((bf16[3072,256]{1,0:T(8,128)(2,1)}, bf16[3072,256]{1,0:T(8,128)(2,1)}, u32[]{:S(2)}, u32[]{:S(2)}) %collective-permute-start) | collective-permute-done | bytes 1572896 | tf_op jit(solution)/shard_map/ppermute | solution.py:150
  263.7 2.7 fusion.60
  270.1 5.0 %all-to-all-start.7 = ((f32[8,72,256]{2,1,0:T(8,128)}), f32[8,72,256]{2,1,0:T(8,128)}, u32[]{:S(2)}, u32[]{:S(2)}) async-start(f32[8,72,256]{2,1,0:T(8,128)} %fusion.64), calls=%async_computation.7 | async-start | bytes 1179648 | tf_op jit(solution)/shard_map/all_to_all | solution.py:25
  275.1 2.7 fusion.62
  277.8 2.8 convolution_add_fusion.3
  280.6 2.7 fusion.56
  283.3 2.7 fusion.58
  286.0 5.9 %all-to-all-done.7 = f32[8,72,256]{2,1,0:T(8,128)} async-done(((f32[8,72,256]{2,1,0:T(8,128)}), f32[8,72,256]{2,1,0:T(8,128)}, u32[]{:S(2)}, u32[]{:S(2)}) %all-to-all-start.7) | async-done | bytes 589856 | tf_op jit(solution)/shard_map/all_to_all | solution.py:25
  295.5 4.4 %all-to-all-start.8 = ((bf16[8,40,2048]{2,1,0:T(8,128)(2,1)}), bf16[8,40,2048]{2,1,0:T(8,128)(2,1)}, u32[]{:S(2)}, u32[]{:S(2)}) async-start(bf16[8,40,2048]{2,1,0:T(8,128)(2,1)} %bitcast.116), calls=%async_computation.9 | async-start | bytes 2621440 | tf_op jit(solution)/shard_map/all_to_all | solution.py:25
  306.1 5.7 %fusion.48 = f32[256,1024]{1,0:T(8,128)} fusion(f32[256,1024]{1,0:T(8,128)S(1)} %add_dynamic-update-slice_fusion, f32[256,256]{1,0:T(8,128)S(1)} %copy-done.15, f32[256,256]{1,0:T(8,128)S(1)} %copy-done.16, f32[256,256]{1,0:T(8,128)S(1)} %copy-done.13, f32[256,256]{1,0:T(8,128)S(1)} %copy-done.14, pred[]{:T(512)S(6)} %eq.1044, ...), kind=kOutput, calls=%fused_computation.80 | convolution fusion | flops 1612972032 | bytes 11010053 | tf_op jit(solution)/shard_map/dot_general | solution.py:21
  311.8 20.3 %all-to-all-done.8 = bf16[8,40,2048]{2,1,0:T(8,128)(2,1)} async-done(((bf16[8,40,2048]{2,1,0:T(8,128)(2,1)}), bf16[8,40,2048]{2,1,0:T(8,128)(2,1)}, u32[]{:S(2)}, u32[]{:S(2)}) %all-to-all-start.8) | async-done | bytes 1310752 | tf_op jit(solution)/shard_map/all_to_all | solution.py:25
  332.1 2.2 fusion.33
  335.5 3.5 all-to-all-start.9
  339.1 7.4 %all-to-all-done.9 = f32[16,16,72]{2,1,0:T(8,128)S(1)} async-done(((f32[16,16,72]{2,1,0:T(8,128)}), f32[16,16,72]{2,1,0:T(8,128)S(1)}, u32[]{:S(2)}, u32[]{:S(2)}) %all-to-all-start.9) | async-done | bytes 73760 | tf_op jit(solution)/shard_map/all_to_all | solution.py:219
  349.6 2.8 fusion.102
  353.2 3.2 fusion.32
  (224 shorter events, 53.1 us)
Async XLA Ops:
  6.5 169.9 %all-gather.5.cloned.1.call-start = ((), (), s32[]{:S(2)}) async-start(), calls=%async_computation.11 | async-start | bytes 7077888 | tf_op jit(solution)/shard_map/all_gather | solution.py:102
  8.9 77.7 %copy-start.2 = (bf16[256,6144]{1,0:T(8,128)(2,1)S(1)}, bf16[256,6144]{1,0:T(8,128)(2,1)}, u32[]{:S(2)}) copy-start(bf16[256,6144]{1,0:T(8,128)(2,1)} %param.10) | copy-start | bytes 9437188
  8.9 181.8 %all-gather.7.cloned.1.call-start = ((), (), s32[]{:S(2)}) async-start(), calls=%async_computation.12 | async-start | bytes 3686400 | tf_op jit(solution)/shard_map/all_gather | solution.py:130
  10.7 81.6 %copy-start.28 = (s32[256]{0:T(256)}, s32[256]{0:T(256)S(1)}, u32[]{:S(2)}) copy-start(s32[256]{0:T(256)S(1)} %select_reduce_fusion.5) | copy-start | bytes 3076
  11.6 77.7 %copy-start.34 = (s32[256]{0:T(256)}, s32[256]{0:T(256)S(1)}, u32[]{:S(2)}) copy-start(s32[256]{0:T(256)S(1)} %get-tuple-element.87) | copy-start | bytes 3076
  78.3 12.5 %copy-start.23 = (s32[16,385]{1,0:T(8,128)}, s32[16,385]{1,0:T(8,128)S(1)}, u32[]{:S(2)}) copy-start(s32[16,385]{1,0:T(8,128)S(1)} %reshape.825) | copy-start | bytes 73924
  95.7 7.0 %copy-start.33 = (s32[8,32]{1,0:T(8,128)S(1)}, s32[8,32]{1,0:T(8,128)}, u32[]{:S(2)}) copy-start(s32[8,32]{1,0:T(8,128)} %get-tuple-element.112) | copy-start | bytes 3076
  95.7 9.6 %copy-start.35 = (s32[256]{0:T(256)S(1)}, s32[256]{0:T(256)}, u32[]{:S(2)}) copy-start(s32[256]{0:T(256)} %copy-done.34) | copy-start | bytes 3076
  95.7 10.2 %copy-start.40 = (s32[256]{0:T(256)S(1)}, s32[256]{0:T(256)}, u32[]{:S(2)}) copy-start(s32[256]{0:T(256)} %get-tuple-element.78) | copy-start | bytes 3076
  95.7 10.2 %copy-start.41 = (s32[256]{0:T(256)S(1)}, s32[256]{0:T(256)}, u32[]{:S(2)}) copy-start(s32[256]{0:T(256)} %get-tuple-element.80) | copy-start | bytes 3076
  95.7 10.8 %copy-start.31 = (s32[256]{0:T(256)S(1)}, s32[256]{0:T(256)}, u32[]{:S(2)}) copy-start(s32[256]{0:T(256)} %copy-done.30) | copy-start | bytes 3076
  95.7 58.6 %all-to-all-start.4 = ((bf16[8,40,2048]{2,1,0:T(8,128)(2,1)}), bf16[8,40,2048]{2,1,0:T(8,128)(2,1)}, u32[]{:S(2)}, u32[]{:S(2)}) async-start(bf16[8,40,2048]{2,1,0:T(8,128)(2,1)} %bitcast.114), calls=%async_computation.4 | async-start | bytes 2621440 | tf_op jit(solution)/shard_map/all_to_all | solution.py:25
  100.0 56.2 %copy-start.19 = (bf16[256,128]{1,0:T(8,128)(2,1)S(1)}, bf16[256,128]{1,0:T(8,128)(2,1)}, u32[]{:S(2)}) copy-start(bf16[256,128]{1,0:T(8,128)(2,1)} %copy-done.18) | copy-start | bytes 196612
  100.0 56.2 %copy-start.21 = (bf16[256,128]{1,0:T(8,128)(2,1)S(1)}, bf16[256,128]{1,0:T(8,128)(2,1)}, u32[]{:S(2)}) copy-start(bf16[256,128]{1,0:T(8,128)(2,1)} %copy-done.20) | copy-start | bytes 196612
  100.0 249.6 %all-gather.9.cloned.1.call-start = ((), (), s32[]{:S(2)}) async-start(), calls=%async_computation.14 | async-start | bytes 2359296 | tf_op jit(solution)/shard_map/all_gather | solution.py:278
  157.1 14.7 %all-to-all-start.5 = ((bf16[8,40,256]{2,1,0:T(8,128)(2,1)}), bf16[8,40,256]{2,1,0:T(8,128)(2,1)S(1)}, u32[]{:S(2)}, u32[]{:S(2)}) async-start(bf16[8,40,256]{2,1,0:T(8,128)(2,1)} %bitcast.17), calls=%async_computation.5 | async-start | bytes 327680 | tf_op jit(solution)/shard_map/all_to_all | solution.py:25
  179.9 86.5 %all-to-all-start.6 = ((bf16[8,40,2048]{2,1,0:T(8,128)(2,1)}), bf16[8,40,2048]{2,1,0:T(8,128)(2,1)}, u32[]{:S(2)}, u32[]{:S(2)}) async-start(bf16[8,40,2048]{2,1,0:T(8,128)(2,1)} %bitcast.115), calls=%async_computation.6 | async-start | bytes 2621440 | tf_op jit(solution)/shard_map/all_to_all | solution.py:25
  188.1 37.5 %collective-permute-start.1 = (bf16[3072,256]{1,0:T(8,128)(2,1)}, bf16[3072,256]{1,0:T(8,128)(2,1)}, u32[]{:S(2)}, u32[]{:S(2)}) collective-permute-start(bf16[3072,256]{1,0:T(8,128)(2,1)} %get-tuple-element.97), channel_id=1, source_target_pairs={{0,16},{16,0},{1,17},{17,1},{2,18},{18,2},{3,19},{19,3},{4,20},{20... | collective-permute-start | bytes 4718600 | tf_op jit(solution)/shard_map/ppermute | solution.py:150
  190.1 68.7 %collective-permute-start = (bf16[3072,256]{1,0:T(8,128)(2,1)}, bf16[3072,256]{1,0:T(8,128)(2,1)}, u32[]{:S(2)}, u32[]{:S(2)}) collective-permute-start(bf16[3072,256]{1,0:T(8,128)(2,1)} %get-tuple-element.98), channel_id=1, source_target_pairs={{0,16},{16,0},{1,17},{17,1},{2,18},{18,2},{3,19},{19,3},{4,20},{20... | collective-permute-start | bytes 4718600 | tf_op jit(solution)/shard_map/ppermute | solution.py:150
  196.9 28.7 %copy-start.11 = (bf16[16,1,128,128]{3,2,1,0:T(8,128)(2,1)S(1)}, bf16[16,1,128,128]{3,2,1,0:T(8,128)(2,1)}, u32[]{:S(2)}) copy-start(bf16[16,1,128,128]{3,2,1,0:T(8,128)(2,1)} %get-tuple-element.104) | copy-start | bytes 1572868
  196.9 61.9 %copy-start.9 = (bf16[16,1,128,128]{3,2,1,0:T(8,128)(2,1)S(1)}, bf16[16,1,128,128]{3,2,1,0:T(8,128)(2,1)}, u32[]{:S(2)}) copy-start(bf16[16,1,128,128]{3,2,1,0:T(8,128)(2,1)} %get-tuple-element.105) | copy-start | bytes 1572868
  225.6 55.0 %collective-permute-start.3 = (bf16[3072,256]{1,0:T(8,128)(2,1)}, bf16[3072,256]{1,0:T(8,128)(2,1)}, u32[]{:S(2)}, u32[]{:S(2)}) collective-permute-start(bf16[3072,256]{1,0:T(8,128)(2,1)} %collective-permute-done.1), channel_id=1, source_target_pairs={{0,2},{2,0},{4,6},{6,4},{8,10},{10,8},{12,14},{14,12},{1,3},{3,1},... | collective-permute-start | bytes 4718600 | tf_op jit(solution)/shard_map/ppermute | solution.py:152
  258.8 24.5 %collective-permute-start.2 = (bf16[3072,256]{1,0:T(8,128)(2,1)}, bf16[3072,256]{1,0:T(8,128)(2,1)}, u32[]{:S(2)}, u32[]{:S(2)}) collective-permute-start(bf16[3072,256]{1,0:T(8,128)(2,1)} %collective-permute-done), channel_id=1, source_target_pairs={{0,2},{2,0},{4,6},{6,4},{8,10},{10,8},{12,14},{14,12},{1,3},{3,1},... | collective-permute-start | bytes 4718600 | tf_op jit(solution)/shard_map/ppermute | solution.py:152
  270.1 7.7 %copy-start.57 = (f32[320,256]{1,0:T(8,128)S(1)}, f32[320,256]{1,0:T(8,128)}, u32[]{:S(2)}) copy-start(f32[320,256]{1,0:T(8,128)} %fusion.52) | copy-start | bytes 983044
  270.1 21.9 %all-to-all-start.7 = ((f32[8,72,256]{2,1,0:T(8,128)}), f32[8,72,256]{2,1,0:T(8,128)}, u32[]{:S(2)}, u32[]{:S(2)}) async-start(f32[8,72,256]{2,1,0:T(8,128)} %fusion.64), calls=%async_computation.7 | async-start | bytes 1179648 | tf_op jit(solution)/shard_map/all_to_all | solution.py:25
  283.3 10.5 %copy-start.32 = (s32[256]{0:T(256)S(1)}, s32[256]{0:T(256)}, u32[]{:S(2)}) copy-start(s32[256]{0:T(256)} %copy-done.30) | copy-start | bytes 3076
  295.5 6.8 %copy-start.27 = (pred[32,256]{1,0:T(32,128)(4,1)S(1)}, pred[32,256]{1,0:T(32,128)(4,1)}, u32[]{:S(2)}) copy-start(pred[32,256]{1,0:T(32,128)(4,1)} %iota_compare_fusion.16) | copy-start | bytes 24580
  295.5 36.6 %all-to-all-start.8 = ((bf16[8,40,2048]{2,1,0:T(8,128)(2,1)}), bf16[8,40,2048]{2,1,0:T(8,128)(2,1)}, u32[]{:S(2)}, u32[]{:S(2)}) async-start(bf16[8,40,2048]{2,1,0:T(8,128)(2,1)} %bitcast.116), calls=%async_computation.9 | async-start | bytes 2621440 | tf_op jit(solution)/shard_map/all_to_all | solution.py:25
  300.0 53.2 %reduce-scatter.2.cloned.1.call-start = ((), (), s32[]{:S(2)}) async-start(), calls=%async_computation.13 | async-start | bytes 1572864 | tf_op jit(solution)/shard_map/reduce_scatter | solution.py:271
  306.1 26.0 %copy-start.24 = (pred[320,256]{1,0:T(32,128)(4,1)S(1)}, pred[320,256]{1,0:T(32,128)(4,1)}, u32[]{:S(2)}) copy-start(pred[320,256]{1,0:T(32,128)(4,1)} %copy.75) | copy-start | bytes 245764
  332.1 6.9 %copy-start.29 = (s32[256]{0:T(256)S(1)}, s32[256]{0:T(256)}, u32[]{:S(2)}) copy-start(s32[256]{0:T(256)} %copy-done.28) | copy-start | bytes 3076
  335.5 11.0 %all-to-all-start.9 = ((f32[16,16,72]{2,1,0:T(8,128)}), f32[16,16,72]{2,1,0:T(8,128)S(1)}, u32[]{:S(2)}, u32[]{:S(2)}) async-start(f32[16,16,72]{2,1,0:T(8,128)} %bitcast.37), calls=%async_computation.10 | async-start | bytes 262144 | tf_op jit(solution)/shard_map/all_to_all | solution.py:219
  (36 other events, 135.7 us)
Sparse Core Ops, SparseCore 0:
  9.0 68.9 all-gather.4
  90.9 61.8 all-gather.6
  154.4 31.9 all-gather.8
  311.9 21.5 reduce-scatter.1

commit v3 on v2

--- a/solution.py
+++ b/solution.py
@@ -80,20 +80,28 @@
     def mask_of(tags):
         return (tags - 1 - me * slots_here)[:, None] == jnp.arange(slots_here)[None, :]
 
-    ints = jnp.concatenate(
-        [
-            tags_of(main_hits),
-            tags_of(extra_hits),
-            tile_pos.reshape(-1),
-            jnp.sum(left.astype(jnp.int32))[None],
-        ]
-    )
-    every = lax.all_gather(ints, ("groups", "pool"), axis=0)
-    any_left = jnp.sum(every[:, -1]) > 0
-    mine = lax.dynamic_slice_in_dim(every, group * pool_width, pool_width, axis=0)
-    main_tags = lax.dynamic_slice_in_dim(mine, me * main_cap, main_cap, axis=1).reshape(-1)
-    extra_tags = mine[:, mains : mains + extra_cap].reshape(-1)
-    all_pos = mine[:, mains + extra_cap : -1].reshape(slot_total, per_shard)
+    common = jnp.concatenate(
+        [tags_of(extra_hits), tile_pos.reshape(-1), jnp.sum(left.astype(jnp.int32))[None]]
+    )
+    every = exchange(
+        jnp.concatenate(
+            [
+                tags_of(main_hits).reshape(pool_width, main_cap),
+                jnp.broadcast_to(common[None, :], (pool_width, common.shape[0])),
+            ],
+            axis=1,
+        )
+    )
+    main_tags = every[:, :main_cap].reshape(-1)
+    extra_tags = every[:, main_cap : main_cap + extra_cap].reshape(-1)
+    all_pos = every[:, main_cap + extra_cap : -1].reshape(slot_total, per_shard)
+    left_count = jnp.sum(every[:, -1])[None]
+    any_left = left_count
+    for step in range(1, group_width):
+        ring = [(g, (g + 1) % group_width) for g in range(group_width)]
+        left_count = lax.ppermute(left_count, "groups", ring)
+        any_left = any_left + left_count
+    any_left = any_left[0] > 0
     main_mask = mask_of(main_tags)
     extra_mask = mask_of(extra_tags)
 
@@ -138,7 +146,6 @@
     half = columns // 2
     quarter = half // 2
     swap = [(p, p ^ 1) for p in range(pool_width)]
-    first_pieces = []
     pieces = [
         lax.dynamic_slice_in_dim(near_weight, core * half + q * quarter, quarter, axis=1)
         for q in range(2)
@@ -148,7 +155,6 @@
         origin = lax.rem(group - step + group_width, group_width)
         feats = lax.dynamic_slice_in_dim(tokens, origin * share, share, axis=1)
         pieces = [lax.ppermute(piece, "groups", ring) for piece in pieces]
-        first_pieces.append(pieces[0])
         others = [lax.ppermute(piece, "pool", swap) for piece in pieces]
         own = [dot(feats, piece) for piece in pieces]
         far = [dot(feats, piece) for piece in others]
@@ -187,7 +193,7 @@
         ],
         axis=1,
     )
-    home = exchange(after(products, received[1], *first_pieces))
+    home = exchange(after(products, received[1]))
     for chunk in range(2, CHUNKS):
         received.append(exchange(after(rows_of(chunk), home)))
     back_hits = jnp.concatenate([main_hits, extra_hits], axis=0)

time: 365 us -> 306 us (0.84)
  blocking collectives: 64.8 us -> 0 us
  local copies, waits for them, and re-layouts: 28.1 us -> 18.6 us
  waiting for transfers between devices: 145 us -> 153 us
  starting transfers between devices: 27.5 us -> 34 us
    unnamed x1 -> x0, blocking collectives: 64.8 us -> none
    ppermute x2, waiting for transfers between devices: 58 us -> 47.6 us  [local(): pieces = [lax.ppermute(piece, 'groups', ring) for piece in pieces]]
    all_gather x1, waiting for transfers between devices: 0.02 us -> 10.2 us  [local(): extra_rows = lax.all_gather(extra_rows, 'pool', axis=0, tiled=True)]
    all_to_all x5 -> x6, waiting for transfers between devices: 79.8 us -> 85.9 us  [exchange(): return lax.all_to_all(x, 'pool', split_axis=0, concat_axis=0, tiled=True)]
    all_to_all x5 -> x6, starting transfers between devices: 21.5 us -> 26.5 us  [exchange(): return lax.all_to_all(x, 'pool', split_axis=0, concat_axis=0, tiled=True)]
  transfers between devices with their start and end apart: 14 -> 16, of which waited for: 7 -> 10; matrix products, arithmetic and copies ran while one was open for 27% -> 30% of each run, Pallas kernels for 0% -> 0%
where the time goes in v3:
time: 306 us; the launch traced here: 304 us
  waiting for transfers between devices  153 us (50%)
  matrix products  49.8 us (16%)
  starting transfers between devices  34 us (11%)
  other arithmetic  29.9 us (10%)
  local copies, waits for them, and re-layouts  18.6 us (6%)
  between operations  18.5 us (6%)
    all_to_all x6, waiting for transfers between devices, exchange(): return lax.all_to_all(x, 'pool', split_axis=0, concat_axis=0, tiled=True)  85.9 us
    ppermute x2, waiting for transfers between devices, local(): pieces = [lax.ppermute(piece, 'groups', ring) for piece in pieces]  47.6 us
    dot_general x23, matrix products, dot(): return jnp.dot(a, b, preferred_element_type=F32)  47.1 us
    all_to_all x6, starting transfers between devices, exchange(): return lax.all_to_all(x, 'pool', split_axis=0, concat_axis=0, tiled=True)  26.5 us
    select_n x2, other arithmetic, local(): picked = jnp.where(row_block[:, None] == block, piece, picked)  11.9 us
    all_gather x1, waiting for transfers between devices, local(): extra_rows = lax.all_gather(extra_rows, 'pool', axis=0, tiled=True)  10.2 us
    all_to_all x1, waiting for transfers between devices, coeff_back(): lax.all_to_all(x.reshape(pool_width * tensor_width, RANK, -1), ('pool', '...  7.21 us
  transfers between devices with their start and end apart: 16, of which 10 were waited for; matrix products, arithmetic and copies ran while one was open for 30% of the time, Pallas kernels for 0%

profile of v3, /device:TPU:0, one launch (start us, length us, event | category | flops | bytes accessed | tf_op | source)
XLA Modules:
  0.0 304.0 jit_solution(18171905059831132663)
XLA Ops:
  12.0 6.3 %all-to-all-start.4 = ((s32[8,1,105]{2,1,0:T(1,128)}), s32[8,1,105]{2,1,0:T(1,128)S(1)}, u32[]{:S(2)}, u32[]{:S(2)}) async-start(s32[8,1,105]{2,1,0:T(1,128)} %bitcast.14), calls=%async_computation.4 | async-start | bytes 8192 | tf_op jit(solution)/shard_map/all_to_all | solution.py:25
  18.3 2.8 convolution_convert_fusion.2
  21.1 2.6 all-to-all-done.4
  26.2 5.9 %select_select_fusion = bf16[256,128]{1,0:T(8,128)(2,1)S(1)} fusion(pred[256]{0:T(512)(128)(4,1)S(1)} %get-tuple-element.225, pred[256]{0:T(512)(128)(4,1)S(1)} %get-tuple-element.180, pred[256]{0:T(512)(128)(4,1)S(1)} %get-tuple-element.181, pred[256]{0:T(512)(128)(4,1)S(1)} %get-tuple-element.182, pred[256]{0:T(512)(128)(4,1)S(1)} %get-tuple-element.183, ...), kind=kLoop, calls=%fused_computation.137 | loop fusion | flops 1572864 | bytes 3223552 | tf_op jit(solution)/shard_map/jit(_where)/select_n | solution.py:131
  32.1 6.0 %select_select_fusion.1 = bf16[256,128]{1,0:T(8,128)(2,1)S(1)} fusion(pred[256]{0:T(512)(128)(4,1)S(1)} %get-tuple-element.237, pred[256]{0:T(512)(128)(4,1)S(1)} %get-tuple-element.282, pred[256]{0:T(512)(128)(4,1)S(1)} %get-tuple-element.281, pred[256]{0:T(512)(128)(4,1)S(1)} %get-tuple-element.280, pred[256]{0:T(512)(128)(4,1)S(1)} %get-tuple-element.279, ...), kind=kLoop, calls=%fused_computation.138 | loop fusion | flops 1572864 | bytes 3223552 | tf_op jit(solution)/shard_map/jit(_where)/select_n | solution.py:131
  39.2 2.8 convolution_convert_fusion.5
  48.3 3.6 %all-to-all-start.5 = ((bf16[8,40,2048]{2,1,0:T(8,128)(2,1)}), bf16[8,40,2048]{2,1,0:T(8,128)(2,1)S(1)}, u32[]{:S(2)}, u32[]{:S(2)}) async-start(bf16[8,40,2048]{2,1,0:T(8,128)(2,1)} %bitcast.16), calls=%async_computation.5 | async-start | bytes 2621440 | tf_op jit(solution)/shard_map/all_to_all | solution.py:25
  57.7 45.4 %all-to-all-done.5 = bf16[8,40,2048]{2,1,0:T(8,128)(2,1)S(1)} async-done(((bf16[8,40,2048]{2,1,0:T(8,128)(2,1)}), bf16[8,40,2048]{2,1,0:T(8,128)(2,1)S(1)}, u32[]{:S(2)}, u32[]{:S(2)}) %all-to-all-start.5) | async-done | bytes 1310752 | tf_op jit(solution)/shard_map/all_to_all | solution.py:25
  105.0 3.4 %all-to-all-start.6 = ((bf16[8,40,256]{2,1,0:T(8,128)(2,1)}), bf16[8,40,256]{2,1,0:T(8,128)(2,1)S(1)}, u32[]{:S(2)}, u32[]{:S(2)}) async-start(bf16[8,40,256]{2,1,0:T(8,128)(2,1)} %bitcast.18), calls=%async_computation.6 | async-start | bytes 327680 | tf_op jit(solution)/shard_map/all_to_all | solution.py:25
  108.4 2.5 fusion.52
  110.9 9.1 %all-to-all-done.6 = bf16[8,40,256]{2,1,0:T(8,128)(2,1)S(1)} async-done(((bf16[8,40,256]{2,1,0:T(8,128)(2,1)}), bf16[8,40,256]{2,1,0:T(8,128)(2,1)S(1)}, u32[]{:S(2)}, u32[]{:S(2)}) %all-to-all-start.6) | async-done | bytes 163872 | tf_op jit(solution)/shard_map/all_to_all | solution.py:25
  121.1 2.2 broadcast_select_fusion.3
  126.3 2.9 fusion.20
  129.1 4.5 %all-to-all-start.7 = ((bf16[8,40,2048]{2,1,0:T(8,128)(2,1)}), bf16[8,40,2048]{2,1,0:T(8,128)(2,1)}, u32[]{:S(2)}, u32[]{:S(2)}) async-start(bf16[8,40,2048]{2,1,0:T(8,128)(2,1)} %bitcast.26), calls=%async_computation.7 | async-start | bytes 2621440 | tf_op jit(solution)/shard_map/all_to_all | solution.py:25
  133.6 3.4 %constant_dynamic-slice_fusion.2 = (bf16[3072,256]{1,0:T(8,128)(2,1)}, bf16[3072,256]{1,0:T(8,128)(2,1)S(1)}) fusion(bf16[3072,1024]{1,0:T(8,128)(2,1)} %all-gather.4.cloned.1.call-done, s32[]{:T(128)S(6)} %select_n.921, s32[]{:T(128)S(6)} %select_n.922), kind=kLoop, calls=%fused_computation.183 | loop fusion | bytes 6291464 | tf_op jit(solution)/shard_map/dynamic_slice | solution.py:150
  139.6 10.2 %all-gather.6.cloned.1.call-done = bf16[256,6400]{1,0:T(8,128)(2,1)} async-done(((bf16[32,6400]{1,0:T(8,128)(2,1)}), bf16[256,6400]{1,0:T(8,128)(2,1)}) %all-gather.6.cloned.1.call-update) | async-done | bytes 3276816 | tf_op jit(solution)/shard_map/all_gather | solution.py:138
  149.9 3.8 %fusion.35 = f32[256,256]{1,0:T(8,128)S(1)} fusion(pred[256,256]{1,0:T(32,128)(4,1)} %copy.95, bf16[6144,256]{1,0:T(8,128)(2,1)} %param.14, bf16[256,6400]{1,0:T(8,128)(2,1)} %all-gather.6.cloned.1.call-done), kind=kOutput, calls=%fused_computation.65 | convolution fusion | flops 805371904 | bytes 6619136 | tf_op jit(solution)/shard_map/dot_general | solution.py:21
  157.0 2.4 broadcast_select_fusion.6
  159.4 15.1 %collective-permute-done = bf16[3072,256]{1,0:T(8,128)(2,1)S(1)} collective-permute-done((bf16[3072,256]{1,0:T(8,128)(2,1)}, bf16[3072,256]{1,0:T(8,128)(2,1)S(1)}, u32[]{:S(2)}, u32[]{:S(2)}) %collective-permute-start) | collective-permute-done | bytes 1572896 | tf_op jit(solution)/shard_map/ppermute | solution.py:157
  174.9 32.6 %collective-permute-done.1 = bf16[3072,256]{1,0:T(8,128)(2,1)} collective-permute-done((bf16[3072,256]{1,0:T(8,128)(2,1)S(1)}, bf16[3072,256]{1,0:T(8,128)(2,1)}, u32[]{:S(2)}, u32[]{:S(2)}) %collective-permute-start.1) | collective-permute-done | bytes 1572896 | tf_op jit(solution)/shard_map/ppermute | solution.py:157
  212.7 5.0 %all-to-all-start.8 = ((f32[8,72,256]{2,1,0:T(8,128)}), f32[8,72,256]{2,1,0:T(8,128)S(1)}, u32[]{:S(2)}, u32[]{:S(2)}) async-start(f32[8,72,256]{2,1,0:T(8,128)} %maximum_add_fusion), calls=%async_computation.8 | async-start | bytes 1179648 | tf_op jit(solution)/shard_map/all_to_all | solution.py:25
  217.8 2.4 fusion.60
  220.2 3.0 convolution_add_fusion.3
  227.3 7.3 %all-to-all-done.8 = f32[8,72,256]{2,1,0:T(8,128)S(1)} async-done(((f32[8,72,256]{2,1,0:T(8,128)}), f32[8,72,256]{2,1,0:T(8,128)S(1)}, u32[]{:S(2)}, u32[]{:S(2)}) %all-to-all-start.8) | async-done | bytes 589856 | tf_op jit(solution)/shard_map/all_to_all | solution.py:25
  235.7 2.8 fusion.21
  238.5 3.7 %all-to-all-start.9 = ((bf16[8,40,2048]{2,1,0:T(8,128)(2,1)}), bf16[8,40,2048]{2,1,0:T(8,128)(2,1)S(1)}, u32[]{:S(2)}, u32[]{:S(2)}) async-start(bf16[8,40,2048]{2,1,0:T(8,128)(2,1)} %bitcast.35), calls=%async_computation.10 | async-start | bytes 2621440 | tf_op jit(solution)/shard_map/all_to_all | solution.py:25
  247.0 5.7 %fusion.48 = f32[256,1024]{1,0:T(8,128)} fusion(f32[256,1024]{1,0:T(8,128)S(1)} %add_dynamic-update-slice_fusion, f32[256,256]{1,0:T(8,128)S(1)} %fusion.56, f32[256,256]{1,0:T(8,128)S(1)} %fusion.58, f32[256,256]{1,0:T(8,128)S(1)} %fusion.60, f32[256,256]{1,0:T(8,128)S(1)} %fusion.62, pred[]{:T(512)S(6)} %eq.1044, ...), kind=kOutput, calls=%fused_computation.80 | convolution fusion | flops 1612972032 | bytes 11010053 | tf_op jit(solution)/shard_map/dot_general | solution.py:21
  252.7 21.6 %all-to-all-done.9 = bf16[8,40,2048]{2,1,0:T(8,128)(2,1)S(1)} async-done(((bf16[8,40,2048]{2,1,0:T(8,128)(2,1)}), bf16[8,40,2048]{2,1,0:T(8,128)(2,1)S(1)}, u32[]{:S(2)}, u32[]{:S(2)}) %all-to-all-start.9) | async-done | bytes 1310752 | tf_op jit(solution)/shard_map/all_to_all | solution.py:25
  277.3 3.7 %all-to-all-start.10 = ((f32[16,16,72]{2,1,0:T(8,128)}), f32[16,16,72]{2,1,0:T(8,128)S(1)}, u32[]{:S(2)}, u32[]{:S(2)}) async-start(f32[16,16,72]{2,1,0:T(8,128)} %bitcast.39), calls=%async_computation.11 | async-start | bytes 262144 | tf_op jit(solution)/shard_map/all_to_all | solution.py:225
  281.1 7.2 %all-to-all-done.10 = f32[16,16,72]{2,1,0:T(8,128)S(1)} async-done(((f32[16,16,72]{2,1,0:T(8,128)}), f32[16,16,72]{2,1,0:T(8,128)S(1)}, u32[]{:S(2)}, u32[]{:S(2)}) %all-to-all-start.10) | async-done | bytes 73760 | tf_op jit(solution)/shard_map/all_to_all | solution.py:225
  290.7 2.8 fusion.100
  294.3 3.2 %fusion.32 = bf16[256,512]{1,0:T(8,128)(2,1)} fusion(f32[256,512]{1,0:T(8,128)} %reduce-scatter.2.cloned.1.call-done, f32[256,512]{1,0:T(8,128)S(1)} %convolution_add_fusion.1, bf16[256,2048]{0,1:T(8,128)(2,1)S(1)} %get-tuple-element.101, bf16[2048,512]{1,0:T(8,128)(2,1)} %all-gather.8.cloned.1.call-done), kind=kOutput, calls=%fused_computation.58 | convolution fusion | flops 537264128 | bytes 4456448 | tf_op jit(solution)/shard_map/dot_general | solution.py:21
  (218 shorter events, 49.6 us)
Async XLA Ops:
  6.5 117.9 %all-gather.4.cloned.1.call-start = ((), (), s32[]{:S(2)}) async-start(), calls=%async_computation.12 | async-start | bytes 7077888 | tf_op jit(solution)/shard_map/all_gather | solution.py:110
  9.0 38.6 %copy-start.22 = (s32[256]{0:T(256)}, s32[256]{0:T(256)S(1)}, u32[]{:S(2)}) copy-start(s32[256]{0:T(256)S(1)} %select_reduce_fusion.5) | copy-start | bytes 3076
  9.3 29.9 %copy-start.24 = (s32[256]{0:T(256)}, s32[256]{0:T(256)S(1)}, u32[]{:S(2)}) copy-start(s32[256]{0:T(256)S(1)} %get-tuple-element.87) | copy-start | bytes 3076
  12.0 11.8 %all-to-all-start.4 = ((s32[8,1,105]{2,1,0:T(1,128)}), s32[8,1,105]{2,1,0:T(1,128)S(1)}, u32[]{:S(2)}, u32[]{:S(2)}) async-start(s32[8,1,105]{2,1,0:T(1,128)} %bitcast.14), calls=%async_computation.4 | async-start | bytes 8192 | tf_op jit(solution)/shard_map/all_to_all | solution.py:25
  18.3 131.6 %all-gather.6.cloned.1.call-start = ((), (), s32[]{:S(2)}) async-start(), calls=%async_computation.13 | async-start | bytes 3686400 | tf_op jit(solution)/shard_map/all_gather | solution.py:138
  23.8 18.2 %copy-start.18 = (s32[8,1,105]{2,1,0:T(1,128)}, s32[8,1,105]{2,1,0:T(1,128)S(1)}, u32[]{:S(2)}) copy-start(s32[8,1,105]{2,1,0:T(1,128)S(1)} %all-to-all-done.4) | copy-start | bytes 10084
  38.1 9.5 %copy-start.14 = (bf16[256,128]{1,0:T(8,128)(2,1)}, bf16[256,128]{1,0:T(8,128)(2,1)S(1)}, u32[]{:S(2)}) copy-start(bf16[256,128]{1,0:T(8,128)(2,1)S(1)} %select_select_fusion.1) | copy-start | bytes 196612
  38.1 9.5 %copy-start.4 = (bf16[16,2,128,128]{3,2,1,0:T(8,128)(2,1)S(1)}, bf16[16,2,128,128]{3,2,1,0:T(8,128)(2,1)}, u32[]{:S(2)}) copy-start(bf16[16,2,128,128]{3,2,1,0:T(8,128)(2,1)} %param.16) | copy-start | bytes 3145732
  39.1 8.5 %copy-start.30 = (s32[256]{0:T(256)}, s32[256]{0:T(256)S(1)}, u32[]{:S(2)}) copy-start(s32[256]{0:T(256)S(1)} %and_select_fusion.2) | copy-start | bytes 3076
  42.7 3.6 %collective-permute-start.4 = (s32[1]{0:T(128)}, s32[1]{0:T(128)}, u32[]{:S(2)}, u32[]{:S(2)}) collective-permute-start(s32[1]{0:T(128)} %bitcast.29), channel_id=1, source_target_pairs={{0,16},{16,0},{1,17},{17,1},{2,18},{18,2},{3,19},{19,3},{4,20},{20... | collective-permute-start | bytes 20 | tf_op jit(solution)/shard_map/ppermute | solution.py:102
  48.3 54.7 %all-to-all-start.5 = ((bf16[8,40,2048]{2,1,0:T(8,128)(2,1)}), bf16[8,40,2048]{2,1,0:T(8,128)(2,1)S(1)}, u32[]{:S(2)}, u32[]{:S(2)}) async-start(bf16[8,40,2048]{2,1,0:T(8,128)(2,1)} %bitcast.16), calls=%async_computation.5 | async-start | bytes 2621440 | tf_op jit(solution)/shard_map/all_to_all | solution.py:25
  51.9 52.2 %copy-start.15 = (bf16[256,128]{1,0:T(8,128)(2,1)S(1)}, bf16[256,128]{1,0:T(8,128)(2,1)}, u32[]{:S(2)}) copy-start(bf16[256,128]{1,0:T(8,128)(2,1)} %copy-done.14) | copy-start | bytes 196612
  51.9 238.8 %all-gather.8.cloned.1.call-start = ((), (), s32[]{:S(2)}) async-start(), calls=%async_computation.15 | async-start | bytes 2359296 | tf_op jit(solution)/shard_map/all_gather | solution.py:284
  54.3 69.0 %copy-start.11 = (bf16[16,1,128,128]{3,2,1,0:T(8,128)(2,1)}, bf16[16,1,128,128]{3,2,1,0:T(8,128)(2,1)S(1)}, u32[]{:S(2)}) copy-start(bf16[16,1,128,128]{3,2,1,0:T(8,128)(2,1)S(1)} %get-tuple-element.104) | copy-start | bytes 1572868
  105.0 15.0 %all-to-all-start.6 = ((bf16[8,40,256]{2,1,0:T(8,128)(2,1)}), bf16[8,40,256]{2,1,0:T(8,128)(2,1)S(1)}, u32[]{:S(2)}, u32[]{:S(2)}) async-start(bf16[8,40,256]{2,1,0:T(8,128)(2,1)} %bitcast.18), calls=%async_computation.6 | async-start | bytes 327680 | tf_op jit(solution)/shard_map/all_to_all | solution.py:25
  129.1 81.0 %all-to-all-start.7 = ((bf16[8,40,2048]{2,1,0:T(8,128)(2,1)}), bf16[8,40,2048]{2,1,0:T(8,128)(2,1)}, u32[]{:S(2)}, u32[]{:S(2)}) async-start(bf16[8,40,2048]{2,1,0:T(8,128)(2,1)} %bitcast.26), calls=%async_computation.7 | async-start | bytes 2621440 | tf_op jit(solution)/shard_map/all_to_all | solution.py:25
  137.0 37.4 %collective-permute-start = (bf16[3072,256]{1,0:T(8,128)(2,1)}, bf16[3072,256]{1,0:T(8,128)(2,1)S(1)}, u32[]{:S(2)}, u32[]{:S(2)}) collective-permute-start(bf16[3072,256]{1,0:T(8,128)(2,1)} %get-tuple-element.97), channel_id=1, source_target_pairs={{0,16},{16,0},{1,17},{17,1},{2,18},{18,2},{3,19},{19,3},{4,20},{20... | collective-permute-start | bytes 4718600 | tf_op jit(solution)/shard_map/ppermute | solution.py:157
  139.0 68.5 %collective-permute-start.1 = (bf16[3072,256]{1,0:T(8,128)(2,1)S(1)}, bf16[3072,256]{1,0:T(8,128)(2,1)}, u32[]{:S(2)}, u32[]{:S(2)}) collective-permute-start(bf16[3072,256]{1,0:T(8,128)(2,1)S(1)} %get-tuple-element.98), channel_id=1, source_target_pairs={{0,16},{16,0},{1,17},{17,1},{2,18},{18,2},{3,19},{19,3},{4,20},{20... | collective-permute-start | bytes 4718600 | tf_op jit(solution)/shard_map/ppermute | solution.py:157
  156.0 18.4 %copy-start.12 = (bf16[16,1,128,128]{3,2,1,0:T(8,128)(2,1)S(1)}, bf16[16,1,128,128]{3,2,1,0:T(8,128)(2,1)}, u32[]{:S(2)}) copy-start(bf16[16,1,128,128]{3,2,1,0:T(8,128)(2,1)} %copy-done.11) | copy-start | bytes 1572868
  156.0 51.5 %copy-start.10 = (bf16[16,1,128,128]{3,2,1,0:T(8,128)(2,1)S(1)}, bf16[16,1,128,128]{3,2,1,0:T(8,128)(2,1)}, u32[]{:S(2)}) copy-start(bf16[16,1,128,128]{3,2,1,0:T(8,128)(2,1)} %get-tuple-element.105) | copy-start | bytes 1572868
  174.4 48.8 %collective-permute-start.2 = (bf16[3072,256]{1,0:T(8,128)(2,1)S(1)}, bf16[3072,256]{1,0:T(8,128)(2,1)}, u32[]{:S(2)}, u32[]{:S(2)}) collective-permute-start(bf16[3072,256]{1,0:T(8,128)(2,1)S(1)} %collective-permute-done), channel_id=1, source_target_pairs={{0,2},{2,0},{4,6},{6,4},{8,10},{10,8},{12,14},{14,12},{1,3},{3,1},... | collective-permute-start | bytes 4718600 | tf_op jit(solution)/shard_map/ppermute | solution.py:158
  207.5 17.8 %collective-permute-start.3 = (bf16[3072,256]{1,0:T(8,128)(2,1)}, bf16[3072,256]{1,0:T(8,128)(2,1)}, u32[]{:S(2)}, u32[]{:S(2)}) collective-permute-start(bf16[3072,256]{1,0:T(8,128)(2,1)} %collective-permute-done.1), channel_id=1, source_target_pairs={{0,2},{2,0},{4,6},{6,4},{8,10},{10,8},{12,14},{14,12},{1,3},{3,1},... | collective-permute-start | bytes 4718600 | tf_op jit(solution)/shard_map/ppermute | solution.py:158
  212.7 7.5 %copy-start.48 = (f32[320,256]{1,0:T(8,128)S(1)}, f32[320,256]{1,0:T(8,128)}, u32[]{:S(2)}) copy-start(f32[320,256]{1,0:T(8,128)} %fusion.52) | copy-start | bytes 983044
  212.7 21.8 %all-to-all-start.8 = ((f32[8,72,256]{2,1,0:T(8,128)}), f32[8,72,256]{2,1,0:T(8,128)S(1)}, u32[]{:S(2)}, u32[]{:S(2)}) async-start(f32[8,72,256]{2,1,0:T(8,128)} %maximum_add_fusion), calls=%async_computation.8 | async-start | bytes 1179648 | tf_op jit(solution)/shard_map/all_to_all | solution.py:25
  225.3 10.4 %copy-start.26 = (s32[256]{0:T(256)S(1)}, s32[256]{0:T(256)}, u32[]{:S(2)}) copy-start(s32[256]{0:T(256)} %copy-done.24) | copy-start | bytes 3076
  238.5 35.8 %all-to-all-start.9 = ((bf16[8,40,2048]{2,1,0:T(8,128)(2,1)}), bf16[8,40,2048]{2,1,0:T(8,128)(2,1)S(1)}, u32[]{:S(2)}, u32[]{:S(2)}) async-start(bf16[8,40,2048]{2,1,0:T(8,128)(2,1)} %bitcast.35), calls=%async_computation.10 | async-start | bytes 2621440 | tf_op jit(solution)/shard_map/all_to_all | solution.py:25
  242.2 52.0 %reduce-scatter.2.cloned.1.call-start = ((), (), s32[]{:S(2)}) async-start(), calls=%async_computation.14 | async-start | bytes 1572864 | tf_op jit(solution)/shard_map/reduce_scatter | solution.py:277
  247.0 27.4 %copy-start.20 = (pred[320,256]{1,0:T(32,128)(4,1)S(1)}, pred[320,256]{1,0:T(32,128)(4,1)}, u32[]{:S(2)}) copy-start(pred[320,256]{1,0:T(32,128)(4,1)} %copy.94) | copy-start | bytes 245764
  247.0 27.4 %copy-start.49 = (f32[320,256]{1,0:T(8,128)S(1)}, f32[320,256]{1,0:T(8,128)}, u32[]{:S(2)}) copy-start(f32[320,256]{1,0:T(8,128)} %convolution_add_fusion.3) | copy-start | bytes 983044
  274.4 14.2 %copy-start.21 = (pred[32,256]{1,0:T(32,128)(4,1)S(1)}, pred[32,256]{1,0:T(32,128)(4,1)}, u32[]{:S(2)}) copy-start(pred[32,256]{1,0:T(32,128)(4,1)} %iota_compare_fusion.16) | copy-start | bytes 24580
  274.4 14.2 %copy-start.28 = (f32[256,16]{0,1:T(8,128)S(1)}, f32[256,16]{0,1:T(8,128)}, u32[]{:S(2)}) copy-start(f32[256,16]{0,1:T(8,128)} %copy-done.27) | copy-start | bytes 49156
  277.3 11.0 %all-to-all-start.10 = ((f32[16,16,72]{2,1,0:T(8,128)}), f32[16,16,72]{2,1,0:T(8,128)S(1)}, u32[]{:S(2)}, u32[]{:S(2)}) async-start(f32[16,16,72]{2,1,0:T(8,128)} %bitcast.39), calls=%async_computation.11 | async-start | bytes 262144 | tf_op jit(solution)/shard_map/all_to_all | solution.py:225
  (34 other events, 127.6 us)
Sparse Core Ops, SparseCore 0:
  9.0 92.7 all-gather.3
  103.4 46.3 all-gather.5
  151.5 37.5 all-gather.7
  252.9 21.5 reduce-scatter.1
